TPU v7x, 512 devices: a whole 4x4x16 slice. The times are simulated.
512 devices in a mesh: row: 16 (over z), col: 32 (over y, x, core).
Axes of the slice: x: 4, y: 4, z: 16, core: 2. Of those that a mesh axis runs over, the one named last changes fastest.
Arguments:
- inputs: bfloat16 [256, 8192], P('col', 'row'), may hold values from -6 to 6
- out_grad: bfloat16 [256, 8192], P('col', 'row'), may hold values from -6 to 6
- w_gate: bfloat16 [8192, 14336], P('row', 'col'), may hold values from -0.0625 to 0.0625
- w_up: bfloat16 [8192, 14336], P('row', 'col'), may hold values from -0.0625 to 0.0625
- w_down: bfloat16 [14336, 8192], P('col', 'row'), may hold values from -0.046875 to 0.046875
Outputs:
- grad_inputs: bfloat16 [256, 8192], P('col', 'row')
- grad_gate: bfloat16 [8192, 14336], P('row', 'col')
- grad_up: bfloat16 [8192, 14336], P('row', 'col')
- grad_down: bfloat16 [14336, 8192], P('col', 'row')
All inputs are finite; a program needn't handle non-finite values.
Results may differ from a plain program's by a relative error of at most 0.0049.
Values may be sent and summed in bfloat16 or wider, within the bound.
No kernel may reach another device: no remote copies, remote signals or barrier semaphores. Data moves between devices by JAX's collectives and lax.ppermute only.
A program may use at most 64 MiB of HBM per device.

v0:
```python
import jax
import jax.numpy as jnp
from jax import lax
from jax.sharding import PartitionSpec as P


def contract(left, right, left_dim, right_dim):
    return lax.dot_general(
        left, right, (((left_dim,), (right_dim,)), ((), ())), preferred_element_type=jnp.float32
    )


def activate(sums, width):
    gate = sums[:, :width]
    up = sums[:, width : 2 * width]
    hidden_grad = sums[:, 2 * width :]
    sigmoid_gate = jax.nn.sigmoid(gate)
    activated = gate * sigmoid_gate
    hidden = (activated * up).astype(jnp.bfloat16)
    up_delta = (hidden_grad * activated).astype(jnp.bfloat16)
    gate_delta = (hidden_grad * up * sigmoid_gate * (1.0 + gate * (1.0 - sigmoid_gate))).astype(
        jnp.bfloat16
    )
    return (hidden, gate_delta, up_delta)


def on_device(inputs, out_grad, w_gate, w_up, w_down):
    full_in, full_grad = (
        lax.all_gather(inputs, "col", axis=0, tiled=True),
        lax.all_gather(out_grad, "col", axis=0, tiled=True),
    )
    width = w_gate.shape[1]
    rows_in = full_in
    rows_grad = full_grad
    sums = lax.psum_scatter(
        jnp.concatenate(
            [
                jnp.dot(rows_in, w_gate, preferred_element_type=jnp.float32),
                jnp.dot(rows_in, w_up, preferred_element_type=jnp.float32),
                contract(rows_grad, w_down, 1, 1),
            ],
            axis=1,
        ),
        "row",
        scatter_dimension=0,
        tiled=True,
    )
    hidden, gate_delta, up_delta = activate(sums, width)
    piece_hidden = lax.all_gather(hidden, "row", axis=0, tiled=True)
    piece_gate = lax.all_gather(gate_delta, "row", axis=0, tiled=True)
    piece_up = lax.all_gather(up_delta, "row", axis=0, tiled=True)
    rows_in = full_in
    rows_grad = full_grad
    acc_down = contract(piece_hidden, rows_grad, 0, 0)
    acc_gate = contract(rows_in, piece_gate, 0, 0)
    acc_up = contract(rows_in, piece_up, 0, 0)
    block_in = contract(piece_gate, w_gate, 1, 1) + contract(piece_up, w_up, 1, 1)
    acc_down, acc_gate, acc_up, acc_in = (acc_down, acc_gate, acc_up, block_in)
    grad_inputs = lax.psum_scatter(acc_in, "col", scatter_dimension=0, tiled=True)
    return (
        grad_inputs.astype(jnp.bfloat16),
        acc_gate.astype(jnp.bfloat16),
        acc_up.astype(jnp.bfloat16),
        acc_down.astype(jnp.bfloat16),
    )


def solution(mesh):
    in_specs = (P("col", "row"), P("col", "row"), P("row", "col"), P("row", "col"), P("col", "row"))
    out_specs = (P("col", "row"), P("row", "col"), P("row", "col"), P("col", "row"))
    return jax.shard_map(
        on_device, mesh=mesh, in_specs=in_specs, out_specs=out_specs, check_vma=False
    )
```

profile of v0, /device:TPU:1, one launch (start us, length us, event | category | flops | bytes accessed | tf_op | source)
XLA Modules:
  0.0 299.1 jit_solution(197472185357648306)
XLA Ops:
  7.2 0.0 copy-start
  7.2 0.0 reduce-scatter.7.cloned.1.call-start
  7.2 29.3 %all_gather.15 = bf16[256,512]{1,0:T(8,128)(2,1)S(1)} all-gather(bf16[8,512]{1,0:T(8,128)(2,1)} %param.5), channel_id=1, replica_groups=mesh['row'=16,'col'=32] {'col'}, dimensions={0}, use_global_device_ids=true | all-gather | bytes 270336 | tf_op jit(solution)/shard_map/all_gather | solution.py:29
  36.5 24.4 %all_gather.16 = bf16[256,512]{1,0:T(8,128)(2,1)S(1)} all-gather(bf16[8,512]{1,0:T(8,128)(2,1)} %param.6), channel_id=1, replica_groups=mesh['row'=16,'col'=32] {'col'}, dimensions={0}, use_global_device_ids=true | all-gather | bytes 270336 | tf_op jit(solution)/shard_map/all_gather | solution.py:30
  60.9 1.3 fusion.4
  62.2 0.3 fusion.3
  62.6 0.3 fusion.5
  62.9 0.1 pad_maximum_fusion
  63.0 1.6 copy.15
  64.5 0.0 reduce-scatter.7.cloned.1.call-update
  64.6 0.0 reduce-scatter.5.cloned.1.call-start
  64.6 59.5 %reduce-scatter.7.cloned.1.call-done = f32[16,1344]{1,0:T(8,128)} async-done(((f32[256,1344]{1,0:T(8,128)}), f32[16,1344]{1,0:T(8,128)}) %reduce-scatter.7.cloned.1.call-update) | async-done | bytes 86032 | tf_op jit(solution)/shard_map/reduce_scatter | solution.py:35
  124.2 0.9 multiply_convert_fusion
  125.1 22.0 %all_gather.18 = bf16[256,448]{1,0:T(8,128)(2,1)S(1)} all-gather(bf16[16,448]{1,0:T(8,128)(2,1)S(1)} %get-tuple-element.5), channel_id=1, replica_groups=mesh['row'=16,'col'=32] {'row'}, dimensions={0}, use_global_device_ids=true | all-gather | bytes 243712 | tf_op jit(solution)/shard_map/all_gather | solution.py:51
  147.1 21.6 %all_gather.17 = bf16[256,448]{1,0:T(8,128)(2,1)S(1)} all-gather(bf16[16,448]{1,0:T(8,128)(2,1)S(1)} %get-tuple-element.6), channel_id=1, replica_groups=mesh['row'=16,'col'=32] {'row'}, dimensions={0}, use_global_device_ids=true | all-gather | bytes 243712 | tf_op jit(solution)/shard_map/all_gather | solution.py:50
  168.6 0.3 fusion.6
  168.9 1.1 convolution_add_fusion
  170.0 0.0 reduce-scatter.5.cloned.1.call-update
  170.0 21.9 %all_gather.19 = bf16[256,448]{1,0:T(8,128)(2,1)S(1)} all-gather(bf16[16,448]{1,0:T(8,128)(2,1)S(1)} %get-tuple-element.4), channel_id=1, replica_groups=mesh['row'=16,'col'=32] {'row'}, dimensions={0}, use_global_device_ids=true | all-gather | bytes 243712 | tf_op jit(solution)/shard_map/all_gather | solution.py:49
  192.0 1.1 fusion
  193.0 1.1 fusion.1
  194.1 1.1 convolution_convert_fusion
  195.2 95.8 %reduce-scatter.5.cloned.1.call-done = f32[8,512]{1,0:T(8,128)} async-done(((f32[256,512]{1,0:T(8,128)}), f32[8,512]{1,0:T(8,128)}) %reduce-scatter.5.cloned.1.call-update) | async-done | bytes 16400 | tf_op jit(solution)/shard_map/reduce_scatter | solution.py:59
  291.0 1.3 convert_element_type.29
  (5 shorter events, 0.0 us)
Async XLA Ops:
  7.2 55.1 %copy-start = (bf16[512,448]{0,1:T(8,128)(2,1)S(1)}, bf16[512,448]{0,1:T(8,128)(2,1)}, u32[]{:S(2)}) copy-start(bf16[512,448]{0,1:T(8,128)(2,1)} %param.7) | copy-start | bytes 1376260
  7.2 117.0 %reduce-scatter.7.cloned.1.call-start = ((), (), s32[]{:S(2)}) async-start(), calls=%async_computation.3 | async-start | bytes 1531904 | tf_op jit(solution)/shard_map/reduce_scatter | solution.py:35
  36.5 26.1 %copy-start.2 = (bf16[448,512]{1,0:T(8,128)(2,1)S(1)}, bf16[448,512]{1,0:T(8,128)(2,1)}, u32[]{:S(2)}) copy-start(bf16[448,512]{1,0:T(8,128)(2,1)} %param.9) | copy-start | bytes 1376260
  64.5 104.4 %copy-start.1 = (bf16[512,448]{0,1:T(8,128)(2,1)S(1)}, bf16[512,448]{0,1:T(8,128)(2,1)}, u32[]{:S(2)}) copy-start(bf16[512,448]{0,1:T(8,128)(2,1)} %param.8) | copy-start | bytes 1376260
  64.6 226.4 %reduce-scatter.5.cloned.1.call-start = ((), (), s32[]{:S(2)}) async-start(), calls=%async_computation.2 | async-start | bytes 540672 | tf_op jit(solution)/shard_map/reduce_scatter | solution.py:59
Sparse Core Ops, SparseCore 0:
  64.7 59.4 reduce-scatter.6
  170.2 120.7 reduce-scatter.4
where the time goes:
time: 300 us; the launch traced here: 299 us
  waiting for transfers between devices  155 us (52%)
  blocking collectives  119 us (40%)
  between operations  14.1 us (5%)
  matrix products  6.56 us (2%)
    reduce_scatter x1, waiting for transfers between devices, on_device(): lax.psum_scatter(acc_in, 'col', scatter_dimension=0, tiled=True)  95.8 us
    reduce_scatter x1, waiting for transfers between devices, on_device(): lax.psum_scatter(jnp.concatenate([jnp.dot(rows_in, w_gate, preferred_elem...  59.5 us
    all_gather x1, blocking collectives, on_device(): lax.all_gather(inputs, 'col', axis=0, tiled=True)  29.3 us
    all_gather x1, blocking collectives, on_device(): lax.all_gather(out_grad, 'col', axis=0, tiled=True)  24.4 us
    all_gather x1, blocking collectives, on_device(): piece_up = lax.all_gather(up_delta, 'row', axis=0, tiled=True)  22 us
    all_gather x1, blocking collectives, on_device(): piece_hidden = lax.all_gather(hidden, 'row', axis=0, tiled=True)  21.9 us
    all_gather x1, blocking collectives, on_device(): piece_gate = lax.all_gather(gate_delta, 'row', axis=0, tiled=True)  21.6 us
  transfers between devices with their start and end apart: 2, of which 2 were waited for; matrix products, arithmetic and copies ran while one was open for 1% of the time, Pallas kernels for 0%

commit v1 on v0

v1 whole, which is shorter than its diff:
```python
import jax
import jax.numpy as jnp
from jax import lax
from jax.sharding import PartitionSpec as P


def contract(left, right, left_dim, right_dim):
    return lax.dot_general(
        left, right, (((left_dim,), (right_dim,)), ((), ())), preferred_element_type=jnp.float32
    )


def activate(sums, width):
    gate = sums[:, :width]
    up = sums[:, width : 2 * width]
    hidden_grad = sums[:, 2 * width :]
    sigmoid_gate = jax.nn.sigmoid(gate)
    activated = gate * sigmoid_gate
    hidden = (activated * up).astype(jnp.bfloat16)
    up_delta = (hidden_grad * activated).astype(jnp.bfloat16)
    gate_delta = (hidden_grad * up * sigmoid_gate * (1.0 + gate * (1.0 - sigmoid_gate))).astype(
        jnp.bfloat16
    )
    return (hidden, gate_delta, up_delta)


def exchange_sum(partial, axis, pieces):
    blocks = partial.reshape(pieces, partial.shape[0] // pieces, partial.shape[1])
    blocks = lax.all_to_all(blocks, axis, 0, 0)
    return jnp.sum(blocks.astype(jnp.float32), axis=0)


def on_device(rows, cols, inputs, out_grad, w_gate, w_up, w_down):
    depth = inputs.shape[1]
    width = w_gate.shape[1]
    both = lax.all_gather(jnp.concatenate([inputs, out_grad], axis=1), "col", axis=0, tiled=True)
    full_in = both[:, :depth]
    full_grad = both[:, depth:]
    partial = jnp.concatenate(
        [
            contract(full_in, w_gate, 1, 0).astype(jnp.bfloat16),
            contract(full_in, w_up, 1, 0).astype(jnp.bfloat16),
            contract(full_grad, w_down, 1, 1).astype(jnp.bfloat16),
        ],
        axis=1,
    )
    sums = exchange_sum(partial, "row", rows)
    hidden, gate_delta, up_delta = activate(sums, width)
    pieces = lax.all_gather(
        jnp.concatenate([gate_delta, up_delta, hidden], axis=1), "row", axis=0, tiled=True
    )
    piece_gate = pieces[:, :width]
    piece_up = pieces[:, width : 2 * width]
    piece_hidden = pieces[:, 2 * width :]
    block_in = contract(piece_gate, w_gate, 1, 1) + contract(piece_up, w_up, 1, 1)
    grad_inputs = exchange_sum(block_in.astype(jnp.bfloat16), "col", cols)
    acc_gate = contract(full_in, piece_gate, 0, 0)
    acc_up = contract(full_in, piece_up, 0, 0)
    acc_down = contract(piece_hidden, full_grad, 0, 0)
    return (
        grad_inputs.astype(jnp.bfloat16),
        acc_gate.astype(jnp.bfloat16),
        acc_up.astype(jnp.bfloat16),
        acc_down.astype(jnp.bfloat16),
    )


def solution(mesh):
    in_specs = (P("col", "row"), P("col", "row"), P("row", "col"), P("row", "col"), P("col", "row"))
    out_specs = (P("col", "row"), P("row", "col"), P("row", "col"), P("col", "row"))

    def step(*arrays):
        return on_device(mesh.shape["row"], mesh.shape["col"], *arrays)

    return jax.shard_map(
        step, mesh=mesh, in_specs=in_specs, out_specs=out_specs, check_vma=False
    )
```

time: 300 us -> 135 us (0.45)
  waiting for transfers between devices: 155 us -> 6.62 us
  blocking collectives: 119 us -> 105 us
  starting transfers between devices: 0.08 us -> 13.7 us
  between operations: 14.1 us -> 0.71 us
    reduce_scatter x2 -> x0, waiting for transfers between devices: 155 us -> none  [the longest x1 95.8 us: on_device(): lax.psum_scatter(acc_in, 'col', scatter_dimension=0, tiled=True)]
    all_gather x5 -> x2, blocking collectives: 119 us -> 56.6 us  [the longest x1 28.6 us: on_device(): lax.all_gather(jnp.concatenate([inputs, out_grad], axis=1), 'col', axis=0...]
    all_to_all x0 -> x1, blocking collectives: none -> 48.4 us  [exchange_sum(): blocks = lax.all_to_all(blocks, axis, 0, 0)]
    all_to_all x0 -> x1, starting transfers between devices: none -> 13.7 us  [exchange_sum(): blocks = lax.all_to_all(blocks, axis, 0, 0)]
    all_to_all x0 -> x1, waiting for transfers between devices: none -> 6.62 us  [exchange_sum(): blocks = lax.all_to_all(blocks, axis, 0, 0)]
    dot_general x6 -> x8, matrix products: 4.92 us -> 6.65 us  [contract(): lax.dot_general(left, right, (((left_dim,), (right_dim,)), ((), ())), pre...]
  transfers between devices with their start and end apart: 2 -> 1, of which waited for: 2 -> 1; matrix products, arithmetic and copies ran while one was open for 1% -> 2% of each run, Pallas kernels for 0% -> 0%
where the time goes in v1:
time: 135 us
  blocking collectives  105 us (78%)
  starting transfers between devices  13.7 us (10%)
  matrix products  6.65 us (5%)
  waiting for transfers between devices  6.62 us (5%)
  other arithmetic  1.65 us (1%)
    all_to_all x1, blocking collectives, exchange_sum(): blocks = lax.all_to_all(blocks, axis, 0, 0)  48.4 us
    all_gather x1, blocking collectives, on_device(): lax.all_gather(jnp.concatenate([inputs, out_grad], axis=1), 'col', axis=0...  28.6 us
    all_gather x1, blocking collectives, on_device(): lax.all_gather(jnp.concatenate([gate_delta, up_delta, hidden], axis=1), '...  28 us
    all_to_all x1, starting transfers between devices, exchange_sum(): blocks = lax.all_to_all(blocks, axis, 0, 0)  13.7 us
    dot_general x8, matrix products, contract(): lax.dot_general(left, right, (((left_dim,), (right_dim,)), ((), ())), pre...  6.65 us
    all_to_all x1, waiting for transfers between devices, exchange_sum(): blocks = lax.all_to_all(blocks, axis, 0, 0)  6.62 us
  transfers between devices with their start and end apart: 1, of which 1 were waited for; matrix products, arithmetic and copies ran while one was open for 2% of the time, Pallas kernels for 0%

profile of v1, /device:TPU:1, one launch (start us, length us, event | category | flops | bytes accessed | tf_op | source)
XLA Modules:
  0.0 134.8 jit_solution(14411840862451234118)
XLA Ops:
  0.6 0.0 copy-start
  0.6 0.8 pad_maximum_fusion.1
  1.4 0.0 copy-start.1
  1.4 28.6 %all_gather.6 = bf16[256,1024]{1,0:T(8,128)(2,1)S(1)} all-gather(bf16[8,1024]{1,0:T(8,128)(2,1)S(1)} %pad_maximum_fusion.1), channel_id=1, replica_groups=mesh['row'=16,'col'=32] {'col'}, dimensions={0}, use_global_device_ids=true | all-gather | bytes 540672 | tf_op jit(solution)/shard_map/all_gather | solution.py:36
  30.0 1.3 convolution_convert_fusion.3
  31.3 0.0 copy-done.1
  31.3 0.3 convolution_convert_fusion.4
  31.7 0.0 copy-done
  31.7 0.3 convolution_convert_fusion.5
  32.0 0.3 copy.9
  32.4 48.4 %all_to_all.10 = bf16[16,16,1344]{2,1,0:T(8,128)(2,1)S(1)} all-to-all(bf16[16,16,1344]{2,1,0:T(8,128)(2,1)S(1)} %bitcast.8), channel_id=1, replica_groups=mesh['row'=16,'col'=32] {'row'}, dimensions={0} | all-to-all | bytes 1376256 | tf_op jit(solution)/shard_map/all_to_all | solution.py:29
  80.8 0.1 convert_reduce_fusion
  80.9 0.1 multiply_convert_fusion
  81.0 0.1 concatenate.11
  81.1 28.0 %all_gather.7 = bf16[256,1344]{1,0:T(8,128)(2,1)S(1)} all-gather(bf16[16,1344]{1,0:T(8,128)(2,1)S(1)} %concatenate.11), channel_id=1, replica_groups=mesh['row'=16,'col'=32] {'row'}, dimensions={0}, use_global_device_ids=true | all-gather | bytes 731136 | tf_op jit(solution)/shard_map/all_gather | solution.py:49
  109.1 0.3 fusion.6
  109.4 1.1 convolution_convert_fusion.2
  110.5 1.0 fusion.1
  111.5 13.7 %all-to-all-start.1 = ((bf16[32,8,512]{2,1,0:T(8,128)(2,1)}), bf16[32,8,512]{2,1,0:T(8,128)(2,1)S(1)}, u32[]{:S(2)}, u32[]{:S(2)}) async-start(bf16[32,8,512]{2,1,0:T(8,128)(2,1)} %fusion.1), calls=%async_computation.1 | async-start | bytes 524288 | tf_op jit(solution)/shard_map/all_to_all | solution.py:29
  125.2 1.2 convolution_convert_fusion.1
  126.4 1.1 convolution_convert_fusion
  127.5 6.6 %all-to-all-done.1 = bf16[32,8,512]{2,1,0:T(8,128)(2,1)S(1)} async-done(((bf16[32,8,512]{2,1,0:T(8,128)(2,1)}), bf16[32,8,512]{2,1,0:T(8,128)(2,1)S(1)}, u32[]{:S(2)}, u32[]{:S(2)}) %all-to-all-start.1) | async-done | bytes 262176 | tf_op jit(solution)/shard_map/all_to_all | solution.py:29
  134.1 0.6 reduce_sum.22
  (1 shorter events, 0.0 us)
Async XLA Ops:
  0.6 31.0 %copy-start = (bf16[512,448]{0,1:T(8,128)(2,1)S(1)}, bf16[512,448]{0,1:T(8,128)(2,1)}, u32[]{:S(2)}) copy-start(bf16[512,448]{0,1:T(8,128)(2,1)} %param.7) | copy-start | bytes 1376260
  1.4 29.9 %copy-start.1 = (bf16[512,448]{0,1:T(8,128)(2,1)S(1)}, bf16[512,448]{0,1:T(8,128)(2,1)}, u32[]{:S(2)}) copy-start(bf16[512,448]{0,1:T(8,128)(2,1)} %param.8) | copy-start | bytes 1376260
  111.5 22.6 %all-to-all-start.1 = ((bf16[32,8,512]{2,1,0:T(8,128)(2,1)}), bf16[32,8,512]{2,1,0:T(8,128)(2,1)S(1)}, u32[]{:S(2)}, u32[]{:S(2)}) async-start(bf16[32,8,512]{2,1,0:T(8,128)(2,1)} %fusion.1), calls=%async_computation.1 | async-start | bytes 524288 | tf_op jit(solution)/shard_map/all_to_all | solution.py:29

commit v2 on v1

--- a/solution.py
+++ b/solution.py
@@ -30,10 +30,15 @@
     return jnp.sum(blocks.astype(jnp.float32), axis=0)
 
 
+def spread(block, axis, pieces):
+    copies = jnp.broadcast_to(block[None], (pieces, *block.shape))
+    return lax.all_to_all(copies, axis, 0, 0).reshape(-1, block.shape[1])
+
+
 def on_device(rows, cols, inputs, out_grad, w_gate, w_up, w_down):
     depth = inputs.shape[1]
     width = w_gate.shape[1]
-    both = lax.all_gather(jnp.concatenate([inputs, out_grad], axis=1), "col", axis=0, tiled=True)
+    both = spread(jnp.concatenate([inputs, out_grad], axis=1), "col", cols)
     full_in = both[:, :depth]
     full_grad = both[:, depth:]
     partial = jnp.concatenate(
@@ -51,9 +56,12 @@
     )
     piece_gate = pieces[:, :width]
     piece_up = pieces[:, width : 2 * width]
+    block_in = contract(piece_gate, w_gate, 1, 1) + contract(piece_up, w_up, 1, 1)
+    block_in, pieces = lax.optimization_barrier((block_in.astype(jnp.bfloat16), pieces))
+    grad_inputs = exchange_sum(block_in, "col", cols)
+    piece_gate = pieces[:, :width]
+    piece_up = pieces[:, width : 2 * width]
     piece_hidden = pieces[:, 2 * width :]
-    block_in = contract(piece_gate, w_gate, 1, 1) + contract(piece_up, w_up, 1, 1)
-    grad_inputs = exchange_sum(block_in.astype(jnp.bfloat16), "col", cols)
     acc_gate = contract(full_in, piece_gate, 0, 0)
     acc_up = contract(full_in, piece_up, 0, 0)
     acc_down = contract(piece_hidden, full_grad, 0, 0)

time: 135 us -> 127 us (0.941)
  blocking collectives: 105 us -> 97.6 us
    all_gather x1 -> x0, blocking collectives: 28.6 us -> none  [on_device(): lax.all_gather(jnp.concatenate([inputs, out_grad], axis=1), 'col', axis=0...]
    all_to_all x0 -> x1, blocking collectives: none -> 21.3 us  [spread(): return lax.all_to_all(copies, axis, 0, 0).reshape(-1, block.shape[1])]
  transfers between devices with their start and end apart: 1 -> 1, of which waited for: 1 -> 1; matrix products, arithmetic and copies ran while one was open for 2% -> 3% of each run, Pallas kernels for 0% -> 0%
where the time goes in v2:
time: 127 us; the launch traced here: 126 us
  blocking collectives  97.6 us (77%)
  starting transfers between devices  14.1 us (11%)
  matrix products  5.63 us (4%)
  waiting for transfers between devices  5.53 us (4%)
  other arithmetic  1.65 us (1%)
    all_to_all x1, blocking collectives, exchange_sum(): blocks = lax.all_to_all(blocks, axis, 0, 0)  47.9 us
    all_gather x1, blocking collectives, on_device(): lax.all_gather(jnp.concatenate([gate_delta, up_delta, hidden], axis=1), '...  28.4 us
    all_to_all x1, blocking collectives, spread(): return lax.all_to_all(copies, axis, 0, 0).reshape(-1, block.shape[1])  21.3 us
    all_to_all x1, starting transfers between devices, exchange_sum(): blocks = lax.all_to_all(blocks, axis, 0, 0)  14.1 us
    dot_general x8, matrix products, contract(): lax.dot_general(left, right, (((left_dim,), (right_dim,)), ((), ())), pre...  5.63 us
    all_to_all x1, waiting for transfers between devices, exchange_sum(): blocks = lax.all_to_all(blocks, axis, 0, 0)  5.53 us
  transfers between devices with their start and end apart: 1, of which 1 were waited for; matrix products, arithmetic and copies ran while one was open for 3% of the time, Pallas kernels for 0%

profile of v2, /device:TPU:1, one launch (start us, length us, event | category | flops | bytes accessed | tf_op | source)
XLA Modules:
  0.0 126.4 jit_solution(11767500895548334089)
XLA Ops:
  0.6 0.0 copy-start
  0.6 0.8 pad_maximum_fusion.1
  1.4 0.0 copy-start.1
  1.5 21.3 %all_to_all.15 = bf16[32,8,1024]{2,1,0:T(8,128)(2,1)S(1)} all-to-all(bf16[32,8,1024]{2,1,0:T(8,128)(2,1)S(1)} %broadcast_in_dim.2), channel_id=1, replica_groups=mesh['row'=16,'col'=32] {'col'}, dimensions={0} | all-to-all | bytes 1048576 | tf_op jit(solution)/shard_map/all_to_all | solution.py:35
  22.8 0.0 copy-done.1
  22.8 0.3 convolution_convert_fusion.4
  23.1 0.7 copy-done.2
  23.8 0.3 convolution_convert_fusion.3
  24.1 0.0 copy-done
  24.1 0.3 convolution_convert_fusion.5
  24.5 0.3 copy.9
  24.9 47.9 %all_to_all.16 = bf16[16,16,1344]{2,1,0:T(8,128)(2,1)S(1)} all-to-all(bf16[16,16,1344]{2,1,0:T(8,128)(2,1)S(1)} %bitcast.14), channel_id=1, replica_groups=mesh['row'=16,'col'=32] {'row'}, dimensions={0} | all-to-all | bytes 1376256 | tf_op jit(solution)/shard_map/all_to_all | solution.py:29
  72.8 0.1 convert_reduce_fusion
  72.9 0.1 multiply_convert_fusion
  73.0 0.1 concatenate.11
  73.1 28.4 %all_gather.3 = bf16[256,1344]{1,0:T(8,128)(2,1)S(1)} all-gather(bf16[16,1344]{1,0:T(8,128)(2,1)S(1)} %concatenate.11), channel_id=1, replica_groups=mesh['row'=16,'col'=32] {'row'}, dimensions={0}, use_global_device_ids=true | all-gather | bytes 731136 | tf_op jit(solution)/shard_map/all_gather | solution.py:54
  101.4 0.3 fusion.2
  101.7 1.0 fusion
  102.8 14.1 %all-to-all-start.2 = ((bf16[32,8,512]{2,1,0:T(8,128)(2,1)}), bf16[32,8,512]{2,1,0:T(8,128)(2,1)S(1)}, u32[]{:S(2)}, u32[]{:S(2)}) async-start(bf16[32,8,512]{2,1,0:T(8,128)(2,1)} %bitcast.2), calls=%async_computation.2 | async-start | bytes 524288 | tf_op jit(solution)/shard_map/all_to_all | solution.py:29
  116.9 1.1 convolution_convert_fusion
  117.9 1.2 convolution_convert_fusion.1
  119.1 1.1 convolution_convert_fusion.2
  120.2 5.5 %all-to-all-done.2 = bf16[32,8,512]{2,1,0:T(8,128)(2,1)S(1)} async-done(((bf16[32,8,512]{2,1,0:T(8,128)(2,1)}), bf16[32,8,512]{2,1,0:T(8,128)(2,1)S(1)}, u32[]{:S(2)}, u32[]{:S(2)}) %all-to-all-start.2) | async-done | bytes 262176 | tf_op jit(solution)/shard_map/all_to_all | solution.py:29
  125.8 0.6 reduce_sum.22
  (3 shorter events, 0.1 us)
Async XLA Ops:
  0.6 23.5 %copy-start = (bf16[512,448]{0,1:T(8,128)(2,1)S(1)}, bf16[512,448]{0,1:T(8,128)(2,1)}, u32[]{:S(2)}) copy-start(bf16[512,448]{0,1:T(8,128)(2,1)} %param.7) | copy-start | bytes 1376260
  1.4 21.4 %copy-start.1 = (bf16[512,448]{0,1:T(8,128)(2,1)S(1)}, bf16[512,448]{0,1:T(8,128)(2,1)}, u32[]{:S(2)}) copy-start(bf16[512,448]{0,1:T(8,128)(2,1)} %param.8) | copy-start | bytes 1376260
  22.8 1.0 copy-start.2
  102.8 23.0 %all-to-all-start.2 = ((bf16[32,8,512]{2,1,0:T(8,128)(2,1)}), bf16[32,8,512]{2,1,0:T(8,128)(2,1)S(1)}, u32[]{:S(2)}, u32[]{:S(2)}) async-start(bf16[32,8,512]{2,1,0:T(8,128)(2,1)} %bitcast.2), calls=%async_computation.2 | async-start | bytes 524288 | tf_op jit(solution)/shard_map/all_to_all | solution.py:29

commit v3 on v2

v3 whole, which is shorter than its diff:
```python
import jax
import jax.numpy as jnp
from jax import lax
from jax.sharding import Mesh
from jax.sharding import PartitionSpec as P

LEAST = -100.0


def contract(left, right, left_dim, right_dim):
    return lax.dot_general(
        left, right, (((left_dim,), (right_dim,)), ((), ())), preferred_element_type=jnp.float32
    )


def activate(gate, up, hidden_grad):
    sigmoid_gate = jax.nn.sigmoid(gate)
    activated = gate * sigmoid_gate
    hidden = (activated * up).astype(jnp.bfloat16)
    up_delta = (hidden_grad * activated).astype(jnp.bfloat16)
    gate_delta = (hidden_grad * up * sigmoid_gate * (1.0 + gate * (1.0 - sigmoid_gate))).astype(
        jnp.bfloat16
    )
    return (hidden, gate_delta, up_delta)


def row_exponent(block):
    largest = jnp.max(jnp.abs(block), axis=1, keepdims=True).astype(jnp.float32)
    return jnp.ceil(jnp.log2(jnp.maximum(largest, 2.0**LEAST)))


def encode(gate, up, hidden_grad, exp_in, exp_grad, shift):
    scale_in = jnp.exp2(shift - exp_in)
    scale_grad = jnp.exp2(shift - exp_grad)
    return jnp.concatenate(
        [
            (gate * scale_in).astype(jnp.float16),
            (up * scale_in).astype(jnp.float16),
            (hidden_grad * scale_grad).astype(jnp.float16),
            exp_in.astype(jnp.float16),
            exp_grad.astype(jnp.float16),
        ],
        axis=1,
    )


def decode(blocks, width, shift):
    blocks = blocks.astype(jnp.float32)
    exp_in = blocks[:, :, 3 * width : 3 * width + 1]
    exp_grad = blocks[:, :, 3 * width + 1 :]
    scale_in = jnp.exp2(exp_in - shift)
    scale_grad = jnp.exp2(exp_grad - shift)
    gate = jnp.sum(blocks[:, :, :width] * scale_in, axis=0)
    up = jnp.sum(blocks[:, :, width : 2 * width] * scale_in, axis=0)
    hidden_grad = jnp.sum(blocks[:, :, 2 * width : 3 * width] * scale_grad, axis=0)
    return gate, up, hidden_grad, jnp.max(exp_in, axis=0), jnp.max(exp_grad, axis=0)


def exchange(array, axis, pieces):
    return lax.all_to_all(array.reshape(pieces, -1, array.shape[1]), axis, 0, 0)


def spread(block, axis, pieces):
    copies = jnp.broadcast_to(block[None], (pieces, *block.shape))
    return lax.all_to_all(copies, axis, 0, 0).reshape(-1, block.shape[1])


def on_device(near, cols, inputs, out_grad, w_gate, w_up, w_down):
    depth = inputs.shape[1]
    width = w_gate.shape[1]
    both = spread(jnp.concatenate([inputs, out_grad], axis=1), "col", cols)
    full_in = both[:, :depth]
    full_grad = both[:, depth:]
    partial = encode(
        contract(full_in, w_gate, 1, 0),
        contract(full_in, w_up, 1, 0),
        contract(full_grad, w_down, 1, 1),
        row_exponent(full_in),
        row_exponent(full_grad),
        9.0,
    )
    sums = decode(exchange(partial, "near", near), width, 9.0)
    sums = decode(lax.all_gather(encode(*sums, 7.0), "far", axis=0), width, 7.0)
    hidden, gate_delta, up_delta = activate(*sums[:3])
    pieces = spread(jnp.concatenate([gate_delta, up_delta, hidden], axis=1), "near", near)
    piece_gate = pieces[:, :width]
    piece_up = pieces[:, width : 2 * width]
    block_in = contract(piece_gate, w_gate, 1, 1) + contract(piece_up, w_up, 1, 1)
    block_in, pieces = lax.optimization_barrier((block_in.astype(jnp.bfloat16), pieces))
    grad_inputs = jnp.sum(exchange(block_in, "col", cols).astype(jnp.float32), axis=0)
    piece_gate = pieces[:, :width]
    piece_up = pieces[:, width : 2 * width]
    piece_hidden = pieces[:, 2 * width :]
    acc_gate = contract(full_in, piece_gate, 0, 0)
    acc_up = contract(full_in, piece_up, 0, 0)
    acc_down = contract(piece_hidden, full_grad, 0, 0)
    return (
        grad_inputs.astype(jnp.bfloat16),
        acc_gate.astype(jnp.bfloat16),
        acc_up.astype(jnp.bfloat16),
        acc_down.astype(jnp.bfloat16),
    )


def solution(mesh):
    rows, cols = mesh.shape["row"], mesh.shape["col"]
    near = 4
    split = Mesh(mesh.devices.reshape(rows // near, near, cols), ("far", "near", "col"))
    row = ("far", "near")
    in_specs = (P("col", row), P("col", row), P(row, "col"), P(row, "col"), P("col", row))
    out_specs = (P("col", row), P(row, "col"), P(row, "col"), P("col", row))

    def step(*arrays):
        return on_device(near, cols, *arrays)

    return jax.shard_map(
        step, mesh=split, in_specs=in_specs, out_specs=out_specs, check_vma=False
    )
```

time: 127 us -> 127 us (level)
  starting transfers between devices: 14.1 us -> 6.09 us
  blocking collectives: 97.6 us -> 103 us
  other arithmetic: 1.65 us -> 3.29 us
  local copies, waits for them, and re-layouts: 1.2 us -> 2.53 us
    all_to_all x1, blocking collectives: 47.9 us -> 22.3 us  [exchange(): return lax.all_to_all(array.reshape(pieces, -1, array.shape[1]), axis, 0, 0)]
    all_to_all x1 -> x2, blocking collectives: 21.3 us -> 45 us  [spread(): return lax.all_to_all(copies, axis, 0, 0).reshape(-1, block.shape[1])]
    all_to_all x1, starting transfers between devices: 14.1 us -> 6.09 us  [exchange(): return lax.all_to_all(array.reshape(pieces, -1, array.shape[1]), axis, 0, 0)]
    all_gather x1, blocking collectives: 28.4 us -> 35.3 us  [on_device(): sums = decode(lax.all_gather(encode(*sums, 7.0), 'far', axis=0), width, 7.0)]
    convert_element_type x0 -> x7, local copies, waits for them, and re-layouts: none -> 1.53 us  [the longest x2 0.36 us: encode(): exp_in.astype(jnp.float16)]
where the time goes in v3:
time: 127 us
  blocking collectives  103 us (81%)
  starting transfers between devices  6.09 us (5%)
  matrix products  5.65 us (4%)
  waiting for transfers between devices  5.53 us (4%)
  other arithmetic  3.29 us (3%)
  local copies, waits for them, and re-layouts  2.53 us (2%)
    all_to_all x2, blocking collectives, spread(): return lax.all_to_all(copies, axis, 0, 0).reshape(-1, block.shape[1])  45 us
    all_gather x1, blocking collectives, on_device(): sums = decode(lax.all_gather(encode(*sums, 7.0), 'far', axis=0), width, 7.0)  35.3 us
    all_to_all x1, blocking collectives, exchange(): return lax.all_to_all(array.reshape(pieces, -1, array.shape[1]), axis, 0, 0)  22.3 us
    all_to_all x1, starting transfers between devices, exchange(): return lax.all_to_all(array.reshape(pieces, -1, array.shape[1]), axis, 0, 0)  6.09 us
    dot_general x8, matrix products, contract(): lax.dot_general(left, right, (((left_dim,), (right_dim,)), ((), ())), pre...  5.65 us
    all_to_all x1, waiting for transfers between devices, exchange(): return lax.all_to_all(array.reshape(pieces, -1, array.shape[1]), axis, 0, 0)  5.53 us
  transfers between devices with their start and end apart: 1, of which 1 were waited for; matrix products, arithmetic and copies ran while one was open for 3% of the time, Pallas kernels for 0%

profile of v3, /device:TPU:1, one launch (start us, length us, event | category | flops | bytes accessed | tf_op | source)
XLA Modules:
  0.0 126.6 jit_solution(7697997742523740775)
XLA Ops:
  0.7 0.8 pad_maximum_fusion
  1.5 21.3 %all_to_all.20 = bf16[32,8,1024]{2,1,0:T(8,128)(2,1)S(1)} all-to-all(bf16[32,8,1024]{2,1,0:T(8,128)(2,1)S(1)} %broadcast_in_dim.4), channel_id=1, replica_groups=mesh['far'=4,'near'=4,'col'=32] {'col'}, dimensions={0} | all-to-all | bytes 1048576 | tf_op jit(solution)/shard_map/all_to_all | solution.py:65
  23.5 0.3 fusion.3
  23.9 0.3 copy.23
  24.2 0.3 fusion.2
  24.5 0.3 copy.22
  24.8 0.3 fusion.1
  25.1 0.3 copy.21
  25.4 0.6 concatenate.23
  26.0 22.3 %all_to_all.21 = f16[4,64,1346]{2,1,0:T(8,128)(2,1)S(1)} all-to-all(f16[4,64,1346]{2,1,0:T(8,128)(2,1)S(1)} %concatenate.23), channel_id=1, replica_groups=mesh['far'=4,'near'=4,'col'=32] {'near'}, dimensions={0} | all-to-all | bytes 1378304 | tf_op jit(solution)/shard_map/all_to_all | solution.py:60
  48.4 0.3 slice_reduce_fusion
  49.0 0.3 fusion.8
  49.7 35.3 %all-gather = f16[256,1346]{1,0:T(8,128)(2,1)S(1)} all-gather(f16[64,1346]{1,0:T(8,128)(2,1)S(1)} %concatenate.24), channel_id=2, replica_groups=mesh['far'=4,'near'=4,'col'=32] {'far'}, dimensions={0}, use_global_device_ids=true | all-gather | bytes 861440 | tf_op jit(solution)/shard_map/all_gather | solution.py:83
  85.1 0.3 fusion.27
  85.3 0.3 fusion.5
  85.9 23.7 %all_to_all.22 = bf16[4,64,1344]{2,1,0:T(8,128)(2,1)S(1)} all-to-all(bf16[4,64,1344]{2,1,0:T(8,128)(2,1)S(1)} %broadcast_in_dim.5), channel_id=1, replica_groups=mesh['far'=4,'near'=4,'col'=32] {'near'}, dimensions={0} | all-to-all | bytes 1376256 | tf_op jit(solution)/shard_map/all_to_all | solution.py:65
  109.6 0.3 fusion.11
  109.9 1.0 fusion
  110.9 6.1 %all-to-all-start.3 = ((bf16[32,8,512]{2,1,0:T(8,128)(2,1)}), bf16[32,8,512]{2,1,0:T(8,128)(2,1)S(1)}, u32[]{:S(2)}, u32[]{:S(2)}) async-start(bf16[32,8,512]{2,1,0:T(8,128)(2,1)} %bitcast.9), calls=%async_computation.3 | async-start | bytes 524288 | tf_op jit(solution)/shard_map/all_to_all | solution.py:60
  117.0 1.1 convolution_convert_fusion
  118.1 1.2 convolution_convert_fusion.1
  119.3 1.1 convolution_convert_fusion.2
  120.4 5.5 %all-to-all-done.3 = bf16[32,8,512]{2,1,0:T(8,128)(2,1)S(1)} async-done(((bf16[32,8,512]{2,1,0:T(8,128)(2,1)}), bf16[32,8,512]{2,1,0:T(8,128)(2,1)S(1)}, u32[]{:S(2)}, u32[]{:S(2)}) %all-to-all-start.3) | async-done | bytes 262176 | tf_op jit(solution)/shard_map/all_to_all | solution.py:60
  125.9 0.6 reduce_sum.72
  (23 shorter events, 1.8 us)
Async XLA Ops:
  0.6 24.1 %copy-start = (bf16[512,448]{0,1:T(8,128)(2,1)S(1)}, bf16[512,448]{0,1:T(8,128)(2,1)}, u32[]{:S(2)}) copy-start(bf16[512,448]{0,1:T(8,128)(2,1)} %param.7) | copy-start | bytes 1376260
  0.6 22.9 %copy-start.2 = (bf16[448,512]{1,0:T(8,128)(2,1)S(1)}, bf16[448,512]{1,0:T(8,128)(2,1)}, u32[]{:S(2)}) copy-start(bf16[448,512]{1,0:T(8,128)(2,1)} %param.9) | copy-start | bytes 1376260
  1.5 22.6 %copy-start.1 = (bf16[512,448]{0,1:T(8,128)(2,1)S(1)}, bf16[512,448]{0,1:T(8,128)(2,1)}, u32[]{:S(2)}) copy-start(bf16[512,448]{0,1:T(8,128)(2,1)} %param.8) | copy-start | bytes 1376260
  110.9 15.0 %all-to-all-start.3 = ((bf16[32,8,512]{2,1,0:T(8,128)(2,1)}), bf16[32,8,512]{2,1,0:T(8,128)(2,1)S(1)}, u32[]{:S(2)}, u32[]{:S(2)}) async-start(bf16[32,8,512]{2,1,0:T(8,128)(2,1)} %bitcast.9), calls=%async_computation.3 | async-start | bytes 524288 | tf_op jit(solution)/shard_map/all_to_all | solution.py:60

commit v4 on v2

v4 whole, which is shorter than its diff:
```python
import jax
import jax.numpy as jnp
from jax import lax
from jax.experimental import pallas as pl
from jax.experimental.pallas import tpu as pltpu
from jax.sharding import Mesh
from jax.sharding import PartitionSpec as P

ROW = ("far", "pair")
LEAST = -100.0
SHIFT = 9.0
NOTE = 64


def contract(left, right, left_dim, right_dim):
    return lax.dot_general(
        left, right, (((left_dim,), (right_dim,)), ((), ())), preferred_element_type=jnp.float32
    )


def activate(gate, up, hidden_grad):
    sigmoid_gate = jax.nn.sigmoid(gate)
    activated = gate * sigmoid_gate
    hidden = (activated * up).astype(jnp.bfloat16)
    up_delta = (hidden_grad * activated).astype(jnp.bfloat16)
    gate_delta = (hidden_grad * up * sigmoid_gate * (1.0 + gate * (1.0 - sigmoid_gate))).astype(
        jnp.bfloat16
    )
    return (hidden, gate_delta, up_delta)


def exchange(array, axis, pieces):
    return lax.all_to_all(array.reshape(pieces, -1, array.shape[-1]), axis, 0, 0)


def spread(block, axis, pieces):
    copies = jnp.broadcast_to(block[None], (pieces, *block.shape))
    return lax.all_to_all(copies, axis, 0, 0).reshape(-1, block.shape[1])


def partial_kernel(both, w_gate, w_up, w_down, sent, kept):
    width, depth = w_gate.shape
    mine = lax.axis_index("pair") == 0
    notes = []
    for i, (w, side) in enumerate(((w_gate, 0), (w_up, 0), (w_down, 1))):
        x = both[:, side * depth : (side + 1) * depth]
        if i != 1:
            largest = jnp.max(jnp.abs(x).astype(jnp.float32), axis=0, keepdims=True)
            largest = jnp.max(largest, axis=1, keepdims=True)
            exp = jnp.ceil(jnp.log2(jnp.maximum(largest, 2.0**LEAST)))
            scale = jnp.exp2(SHIFT - exp)
            notes.append(jnp.broadcast_to(exp, (sent.shape[0], NOTE // 2)))
        part = contract(x, w[...], 1, 1).reshape(-1, 2, 8, width)
        even = part[:, 0].reshape(-1, width)
        odd = part[:, 1].reshape(-1, width)
        at = pl.ds(i * width, width)
        kept[:, at] = jnp.where(mine, even, odd)
        sent[:, at] = (jnp.where(mine, odd, even) * scale).astype(sent.dtype)
    sent[:, 3 * width :] = jnp.concatenate(notes, axis=1).astype(sent.dtype)


def partial_sums(both, w_gate, w_up, w_down):
    tokens, width = both.shape[0], w_gate.shape[0]
    return pl.pallas_call(
        partial_kernel,
        out_shape=(
            jax.ShapeDtypeStruct((tokens // 2, 3 * width + NOTE), jnp.float32),
            jax.ShapeDtypeStruct((tokens // 2, 3 * width), jnp.float32),
        ),
        in_specs=[pl.BlockSpec(memory_space=pltpu.VMEM)] * 4,
        out_specs=[pl.BlockSpec(memory_space=pltpu.VMEM)] * 2,
        compiler_params=pltpu.CompilerParams(vmem_limit_bytes=16 << 20),
        name="partial_sums",
    )(both, w_gate, w_up, w_down)


def fold_kernel(got, kept, out):
    theirs = got[1 - lax.axis_index("pair")]
    width = kept.shape[1] // 3
    at = 3 * width
    scale_in = jnp.exp2(theirs[:, at : at + 1] - SHIFT)
    scale_grad = jnp.exp2(theirs[:, at + NOTE // 2 : at + NOTE // 2 + 1] - SHIFT)
    column = lax.broadcasted_iota(jnp.int32, kept.shape, 1)
    scale = jnp.where(column < 2 * width, scale_in, scale_grad)
    out[...] = (kept[...] + theirs[:, :at] * scale).astype(out.dtype)


def fold(sent, kept):
    got = lax.all_gather(sent.astype(jnp.float16), "pair", axis=0).astype(jnp.float32)
    return pl.pallas_call(
        fold_kernel,
        out_shape=jax.ShapeDtypeStruct(kept.shape, jnp.bfloat16),
        in_specs=[pl.BlockSpec(memory_space=pltpu.VMEM)] * 2,
        out_specs=pl.BlockSpec(memory_space=pltpu.VMEM),
        compiler_params=pltpu.CompilerParams(vmem_limit_bytes=16 << 20),
        name="fold",
    )(got, kept)


def block_kernel(pieces, w_gate, w_up, out):
    width = w_gate.shape[0]
    total = contract(pieces[:, :width], w_gate[...], 1, 0)
    total += contract(pieces[:, width : 2 * width], w_up[...], 1, 0)
    out[...] = total.astype(out.dtype)


def block_inputs(pieces, w_gate, w_up):
    return pl.pallas_call(
        block_kernel,
        out_shape=jax.ShapeDtypeStruct((pieces.shape[0], w_gate.shape[1]), jnp.bfloat16),
        in_specs=[pl.BlockSpec(memory_space=pltpu.VMEM)] * 3,
        out_specs=pl.BlockSpec(memory_space=pltpu.VMEM),
        compiler_params=pltpu.CompilerParams(vmem_limit_bytes=16 << 20),
        name="block_inputs",
    )(pieces, w_gate, w_up)


def on_device(rows, cols, inputs, out_grad, w_gate, w_up, w_down):
    depth = inputs.shape[1]
    width = w_gate.shape[1]
    both = spread(jnp.concatenate([inputs, out_grad], axis=1), "col", cols)
    full_in = both[:, :depth]
    full_grad = both[:, depth:]
    partial = fold(*partial_sums(both, w_gate.T, w_up.T, w_down))
    blocks = exchange(partial, ROW, rows).astype(jnp.float32)
    sums = jnp.sum(blocks.reshape(rows // 2, 2, *blocks.shape[1:]), axis=0)
    sums = sums.reshape(-1, sums.shape[-1])
    hidden, gate_delta, up_delta = activate(
        sums[:, :width], sums[:, width : 2 * width], sums[:, 2 * width :]
    )
    pieces = lax.all_gather(
        jnp.concatenate([gate_delta, up_delta, hidden], axis=1), ROW, axis=0, tiled=True
    )
    block_in = block_inputs(pieces, w_gate.T, w_up.T)
    block_in, pieces = lax.optimization_barrier((block_in, pieces))
    grad_inputs = jnp.sum(exchange(block_in, "col", cols).astype(jnp.float32), axis=0)
    piece_gate = pieces[:, :width]
    piece_up = pieces[:, width : 2 * width]
    piece_hidden = pieces[:, 2 * width :]
    acc_gate = contract(full_in, piece_gate, 0, 0)
    acc_up = contract(full_in, piece_up, 0, 0)
    acc_down = contract(piece_hidden, full_grad, 0, 0)
    return (
        grad_inputs.astype(jnp.bfloat16),
        acc_gate.astype(jnp.bfloat16),
        acc_up.astype(jnp.bfloat16),
        acc_down.astype(jnp.bfloat16),
    )


def solution(mesh):
    rows, cols = mesh.shape["row"], mesh.shape["col"]
    split = Mesh(mesh.devices.reshape(rows // 2, 2, cols), (*ROW, "col"))
    in_specs = (P("col", ROW), P("col", ROW), P(ROW, "col"), P(ROW, "col"), P("col", ROW))
    out_specs = (P("col", ROW), P(ROW, "col"), P(ROW, "col"), P("col", ROW))

    def step(*arrays):
        return on_device(rows, cols, *arrays)

    return jax.shard_map(
        step, mesh=split, in_specs=in_specs, out_specs=out_specs, check_vma=False
    )
```

time: 127 us -> 120 us (0.945)
  blocking collectives: 97.6 us -> 92 us
  matrix products: 5.63 us -> 3.36 us
  Pallas kernels: 0 us -> 1.91 us
    all_to_all x1, blocking collectives: 47.9 us -> 28.9 us  [exchange(): lax.all_to_all(array.reshape(pieces, -1, array.shape[-1]), axis, 0, 0)]
    all_gather x1 -> x2, blocking collectives: 28.4 us -> 41.8 us  [the longest x1 31.6 us: on_device(): lax.all_gather(jnp.concatenate([gate_delta, up_delta, hidden], axis=1), R...]
    dot_general x8 -> x3, matrix products: 5.63 us -> 3.36 us  [contract(): lax.dot_general(left, right, (((left_dim,), (right_dim,)), ((), ())), pre...]
    pallas_call x0 -> x3, Pallas kernels: none -> 1.91 us  [the longest x1 1.16 us: block_inputs(): pl.pallas_call(block_kernel, out_shape=jax.ShapeDtypeStruct((pieces.shape...]
where the time goes in v4:
time: 120 us
  blocking collectives  92 us (77%)
  starting transfers between devices  14.7 us (12%)
  waiting for transfers between devices  5.53 us (5%)
  matrix products  3.36 us (3%)
  Pallas kernels  1.91 us (2%)
  other arithmetic  1.74 us (1%)
    all_gather x1, blocking collectives, on_device(): lax.all_gather(jnp.concatenate([gate_delta, up_delta, hidden], axis=1), R...  31.6 us
    all_to_all x1, blocking collectives, exchange(): lax.all_to_all(array.reshape(pieces, -1, array.shape[-1]), axis, 0, 0)  28.9 us
    all_to_all x1, blocking collectives, spread(): return lax.all_to_all(copies, axis, 0, 0).reshape(-1, block.shape[1])  21.2 us
    all_to_all x1, starting transfers between devices, exchange(): lax.all_to_all(array.reshape(pieces, -1, array.shape[-1]), axis, 0, 0)  14.7 us
    all_gather x1, blocking collectives, fold(): lax.all_gather(sent.astype(jnp.float16), 'pair', axis=0).astype(jnp.float32)  10.2 us
    all_to_all x1, waiting for transfers between devices, exchange(): lax.all_to_all(array.reshape(pieces, -1, array.shape[-1]), axis, 0, 0)  5.53 us
    dot_general x3, matrix products, contract(): lax.dot_general(left, right, (((left_dim,), (right_dim,)), ((), ())), pre...  3.36 us
  transfers between devices with their start and end apart: 1, of which 1 were waited for; matrix products, arithmetic and copies ran while one was open for 3% of the time, Pallas kernels for 0%

profile of v4, /device:TPU:1, one launch (start us, length us, event | category | flops | bytes accessed | tf_op | source)
XLA Modules:
  0.0 120.1 jit_solution(14390476844220509496)
XLA Ops:
  0.6 0.0 copy-start.2
  0.6 0.0 copy-start.1
  0.7 0.0 copy-start
  0.7 0.8 pad_maximum_fusion
  1.5 0.1 broadcast_in_dim.2
  1.5 21.2 %all_to_all.15 = bf16[32,8,1024]{2,1,0:T(8,128)(2,1)S(1)} all-to-all(bf16[32,8,1024]{2,1,0:T(8,128)(2,1)S(1)} %broadcast_in_dim.2), channel_id=1, replica_groups=mesh['far'=8,'pair'=2,'col'=32] {'col'}, dimensions={0} | all-to-all | bytes 1048576 | tf_op jit(solution)/shard_map/all_to_all | solution.py:38
  22.7 0.0 copy-done.2
  22.7 0.0 copy-done
  22.7 0.6 partial_sums.1
  23.4 10.2 %all-gather = f16[256,1408]{1,0:T(8,128)(2,1)S(1)} all-gather(f16[128,1408]{1,0:T(8,128)(2,1)S(1)} %convert_element_type.27), channel_id=2, replica_groups=mesh['far'=8,'pair'=2,'col'=32] {'pair'}, dimensions={0}, use_global_device_ids=true | all-gather | bytes 1081344 | tf_op jit(solution)/shard_map/all_gather | solution.py:89
  33.6 0.1 convert.2.got
  33.7 0.1 fold.1
  33.9 28.9 %all_to_all.16 = bf16[16,8,1344]{2,1,0:T(8,128)(2,1)S(1)} all-to-all(bf16[16,8,1344]{2,1,0:T(8,128)(2,1)S(1)} %bitcast.18), channel_id=1, replica_groups=mesh['far'=8,'pair'=2,'col'=32] {'far','pair'}, dimensions={0} | all-to-all | bytes 688128 | tf_op jit(solution)/shard_map/all_to_all | solution.py:33
  62.8 0.1 convert_reduce_fusion
  62.9 0.1 multiply_convert_fusion
  62.9 0.1 concatenate.7
  63.0 31.6 %all_gather.11.pieces = bf16[256,1344]{1,0:T(8,128)(2,1)S(1)} all-gather(bf16[16,1344]{1,0:T(8,128)(2,1)S(1)} %concatenate.7), channel_id=1, replica_groups=mesh['far'=8,'pair'=2,'col'=32] {'far','pair'}, dimensions={0}, use_global_device_ids=true | all-gather | bytes 731136 | tf_op jit(solution)/shard_map/all_gather | solution.py:131
  94.7 1.2 block_inputs.1
  95.8 14.7 %all-to-all-start.2 = ((bf16[32,8,512]{2,1,0:T(8,128)(2,1)}), bf16[32,8,512]{2,1,0:T(8,128)(2,1)S(1)}, u32[]{:S(2)}, u32[]{:S(2)}) async-start(bf16[32,8,512]{2,1,0:T(8,128)(2,1)} %bitcast.7), calls=%async_computation.2 | async-start | bytes 524288 | tf_op jit(solution)/shard_map/all_to_all | solution.py:33
  110.6 1.1 convolution_convert_fusion
  111.6 1.2 convolution_convert_fusion.1
  112.8 1.1 convolution_convert_fusion.2
  113.9 5.5 %all-to-all-done.2 = bf16[32,8,512]{2,1,0:T(8,128)(2,1)S(1)} async-done(((bf16[32,8,512]{2,1,0:T(8,128)(2,1)}), bf16[32,8,512]{2,1,0:T(8,128)(2,1)S(1)}, u32[]{:S(2)}, u32[]{:S(2)}) %all-to-all-start.2) | async-done | bytes 262176 | tf_op jit(solution)/shard_map/all_to_all | solution.py:33
  119.5 0.6 reduce_sum.22
  (2 shorter events, 0.0 us)
Async XLA Ops:
  0.6 22.1 %copy-start.2 = (bf16[448,512]{1,0:T(8,128)(2,1)S(1)}, bf16[448,512]{1,0:T(8,128)(2,1)}, u32[]{:S(2)}) copy-start(bf16[448,512]{1,0:T(8,128)(2,1)} %w_down.1) | copy-start | bytes 1376260
  0.6 22.1 %copy-start.1 = (bf16[512,448]{0,1:T(8,128)(2,1)S(1)}, bf16[512,448]{0,1:T(8,128)(2,1)}, u32[]{:S(2)}) copy-start(bf16[512,448]{0,1:T(8,128)(2,1)} %param.8) | copy-start | bytes 1376260
  0.7 22.1 %copy-start = (bf16[512,448]{0,1:T(8,128)(2,1)S(1)}, bf16[512,448]{0,1:T(8,128)(2,1)}, u32[]{:S(2)}) copy-start(bf16[512,448]{0,1:T(8,128)(2,1)} %param.7) | copy-start | bytes 1376260
  95.8 23.6 %all-to-all-start.2 = ((bf16[32,8,512]{2,1,0:T(8,128)(2,1)}), bf16[32,8,512]{2,1,0:T(8,128)(2,1)S(1)}, u32[]{:S(2)}, u32[]{:S(2)}) async-start(bf16[32,8,512]{2,1,0:T(8,128)(2,1)} %bitcast.7), calls=%async_computation.2 | async-start | bytes 524288 | tf_op jit(solution)/shard_map/all_to_all | solution.py:33

commit v5 on v4

v5 whole, which is shorter than its diff:
```python
import jax
import jax.numpy as jnp
from jax import lax
from jax.experimental import pallas as pl
from jax.experimental.pallas import tpu as pltpu
from jax.sharding import Mesh
from jax.sharding import PartitionSpec as P

ROW = ("far", "pair")
LEAST = -100.0
SHIFT = 9.0
PAIR_SHIFT = 8.0
NOTE = 64


def contract(left, right, left_dim, right_dim):
    return lax.dot_general(
        left, right, (((left_dim,), (right_dim,)), ((), ())), preferred_element_type=jnp.float32
    )


def activate(gate, up, hidden_grad):
    sigmoid_gate = jax.nn.sigmoid(gate)
    activated = gate * sigmoid_gate
    hidden = (activated * up).astype(jnp.bfloat16)
    up_delta = (hidden_grad * activated).astype(jnp.bfloat16)
    gate_delta = (hidden_grad * up * sigmoid_gate * (1.0 + gate * (1.0 - sigmoid_gate))).astype(
        jnp.bfloat16
    )
    return (hidden, gate_delta, up_delta)


def exchange(array, axis, pieces):
    return lax.all_to_all(array.reshape(pieces, -1, array.shape[-1]), axis, 0, 0)


def spread(block, axis, pieces):
    copies = jnp.broadcast_to(block[None], (pieces, *block.shape))
    return lax.all_to_all(copies, axis, 0, 0).reshape(-1, block.shape[1])


def partial_kernel(both, w_gate, w_up, w_down, sent, kept):
    width, depth = w_gate.shape
    mine = lax.axis_index("pair") == 0
    notes = []
    for i, (w, side) in enumerate(((w_gate, 0), (w_up, 0), (w_down, 1))):
        x = both[:, side * depth : (side + 1) * depth]
        if i != 1:
            largest = jnp.max(jnp.abs(x).astype(jnp.float32), axis=0, keepdims=True)
            largest = jnp.max(largest, axis=1, keepdims=True)
            exp = jnp.ceil(jnp.log2(jnp.maximum(largest, 2.0**LEAST)))
            scale = jnp.exp2(SHIFT - exp)
            notes.append(jnp.broadcast_to(exp, (sent.shape[0], NOTE // 2)))
        part = contract(x, w[...], 1, 1).reshape(-1, 2, 8, width)
        even = part[:, 0].reshape(-1, width)
        odd = part[:, 1].reshape(-1, width)
        at = pl.ds(i * width, width)
        kept[:, at] = jnp.where(mine, even, odd)
        sent[:, at] = jnp.where(mine, odd, even) * scale
    notes = jnp.concatenate(notes, axis=1)
    kept[:, 3 * width :] = notes
    sent[:, 3 * width :] = notes


def partial_sums(both, w_gate, w_up, w_down):
    tokens, width = both.shape[0], w_gate.shape[0]
    return pl.pallas_call(
        partial_kernel,
        out_shape=[jax.ShapeDtypeStruct((tokens // 2, 3 * width + NOTE), jnp.float32)] * 2,
        in_specs=[pl.BlockSpec(memory_space=pltpu.VMEM)] * 4,
        out_specs=[pl.BlockSpec(memory_space=pltpu.VMEM)] * 2,
        compiler_params=pltpu.CompilerParams(vmem_limit_bytes=16 << 20),
        name="partial_sums",
    )(both, w_gate, w_up, w_down)


def exponents(block):
    at = block.shape[-1] - NOTE
    return block[..., at : at + 1], block[..., at + NOTE // 2 : at + NOTE // 2 + 1]


def fold_kernel(got, kept, out):
    theirs, mine = got[1 - lax.axis_index("pair")], kept[...]
    at = mine.shape[1] - NOTE
    column = lax.broadcasted_iota(jnp.int32, (mine.shape[0], at), 1)
    grads = column >= 2 * (at // 3)
    got_in, got_grad = exponents(theirs)
    own_in, own_grad = exponents(mine)
    exp_in, exp_grad = jnp.maximum(got_in, own_in), jnp.maximum(got_grad, own_grad)
    scale = jnp.where(grads, jnp.exp2(got_grad - SHIFT), jnp.exp2(got_in - SHIFT))
    total = mine[:, :at] + theirs[:, :at] * scale
    scale = jnp.where(grads, jnp.exp2(PAIR_SHIFT - exp_grad), jnp.exp2(PAIR_SHIFT - exp_in))
    out[:, :at] = total * scale
    note = (mine.shape[0], NOTE // 2)
    out[:, at:] = jnp.concatenate(
        [jnp.broadcast_to(exp_in, note), jnp.broadcast_to(exp_grad, note)], axis=1
    )


def fold(sent, kept):
    got = lax.all_gather(sent.astype(jnp.float16), "pair", axis=0).astype(jnp.float32)
    return pl.pallas_call(
        fold_kernel,
        out_shape=jax.ShapeDtypeStruct(kept.shape, jnp.float32),
        in_specs=[pl.BlockSpec(memory_space=pltpu.VMEM)] * 2,
        out_specs=pl.BlockSpec(memory_space=pltpu.VMEM),
        compiler_params=pltpu.CompilerParams(vmem_limit_bytes=16 << 20),
        name="fold",
    )(got, kept)


def activate_kernel(blocks, out):
    width = (blocks.shape[2] - NOTE) // 3
    stride = out.shape[2] // 2
    for h in range(2):
        sums = [0.0, 0.0]
        for s in range(h, blocks.shape[0], 2):
            block = blocks[s]
            parts = block[:, : 2 * width], block[:, 2 * width : 3 * width]
            for i, exp in enumerate(exponents(block)):
                sums[i] += parts[i] * jnp.exp2(exp - PAIR_SHIFT)
        hidden, gate_delta, up_delta = activate(sums[0][:, :width], sums[0][:, width:], sums[1])
        pad = jnp.zeros((hidden.shape[0], stride - 3 * width), out.dtype)
        out[0, :, h * stride : (h + 1) * stride] = jnp.concatenate(
            [gate_delta, up_delta, hidden, pad], axis=1
        )


def activations(blocks):
    stride = -(-blocks.shape[2] // 128) * 128
    return pl.pallas_call(
        activate_kernel,
        out_shape=jax.ShapeDtypeStruct((1, blocks.shape[1], 2 * stride), jnp.bfloat16),
        in_specs=[pl.BlockSpec(memory_space=pltpu.VMEM)],
        out_specs=pl.BlockSpec(memory_space=pltpu.VMEM),
        compiler_params=pltpu.CompilerParams(vmem_limit_bytes=16 << 20),
        name="activations",
    )(blocks)


def piece(pieces, h, which, width):
    stride = pieces.shape[2] // 2
    at = h * stride + which * width
    return pieces[:, :, at : at + width].reshape(-1, width)


def block_kernel(pieces, w_gate, w_up, out):
    width = w_gate.shape[0]
    for h in range(2):
        total = contract(piece(pieces, h, 0, width), w_gate[...], 1, 0)
        total += contract(piece(pieces, h, 1, width), w_up[...], 1, 0)
        out[:, h] = total.reshape(out.shape[0], *out.shape[2:]).astype(out.dtype)


def block_inputs(pieces, w_gate, w_up):
    return pl.pallas_call(
        block_kernel,
        out_shape=jax.ShapeDtypeStruct(
            (pieces.shape[0], 2, pieces.shape[1], w_gate.shape[1]), jnp.bfloat16
        ),
        in_specs=[pl.BlockSpec(memory_space=pltpu.VMEM)] * 3,
        out_specs=pl.BlockSpec(memory_space=pltpu.VMEM),
        compiler_params=pltpu.CompilerParams(vmem_limit_bytes=16 << 20),
        name="block_inputs",
    )(pieces, w_gate, w_up)


def grad_kernel(both, pieces, grad_gate, grad_up, grad_down):
    width, depth = grad_gate.shape
    for which, side, out in ((0, 0, grad_gate), (1, 0, grad_up), (2, 1, grad_down)):
        total = None
        for h in range(2):
            x = both[:, h, :, side * depth : (side + 1) * depth].reshape(-1, depth)
            term = contract(piece(pieces, h, which, width), x, 0, 0)
            total = term if total is None else total + term
        out[...] = total.astype(out.dtype)


def weight_grads(both, pieces, width):
    depth = both.shape[1] // 2
    both = both.reshape(pieces.shape[0], 2, pieces.shape[1], 2 * depth)
    return pl.pallas_call(
        grad_kernel,
        out_shape=[jax.ShapeDtypeStruct((width, depth), jnp.bfloat16)] * 3,
        in_specs=[pl.BlockSpec(memory_space=pltpu.VMEM)] * 2,
        out_specs=[pl.BlockSpec(memory_space=pltpu.VMEM)] * 3,
        compiler_params=pltpu.CompilerParams(vmem_limit_bytes=16 << 20),
        cost_estimate=pl.CostEstimate(flops=6 * 256 * 448 * 512, bytes_accessed=4 << 20, transcendentals=0),
        name="weight_grads",
    )(both, pieces)


def sum_kernel(blocks, out):
    out[...] = jnp.sum(blocks[...].astype(jnp.float32), axis=0).astype(out.dtype)


def final_sum(blocks):
    return pl.pallas_call(
        sum_kernel,
        out_shape=jax.ShapeDtypeStruct(blocks.shape[1:], jnp.bfloat16),
        in_specs=[pl.BlockSpec(memory_space=pltpu.VMEM)],
        out_specs=pl.BlockSpec(memory_space=pltpu.VMEM),
        compiler_params=pltpu.CompilerParams(vmem_limit_bytes=16 << 20),
        name="final_sum",
    )(blocks)


def on_device(rows, cols, inputs, out_grad, w_gate, w_up, w_down):
    width = w_gate.shape[1]
    both = spread(jnp.concatenate([inputs, out_grad], axis=1), "col", cols)
    partial = fold(*partial_sums(both, w_gate.T, w_up.T, w_down))
    blocks = exchange(partial.astype(jnp.float16), ROW, rows).astype(jnp.float32)
    payload = activations(blocks)
    pieces = lax.all_gather(payload, ROW, axis=0, tiled=True)
    block_in = block_inputs(pieces, w_gate.T, w_up.T).reshape(both.shape[0], -1)
    block_in, pieces = lax.optimization_barrier((block_in, pieces))
    grad_inputs = final_sum(exchange(block_in, "col", cols))
    grad_gate, grad_up, grad_down = weight_grads(both, pieces, width)
    return (grad_inputs, grad_gate.T, grad_up.T, grad_down)


def solution(mesh):
    rows, cols = mesh.shape["row"], mesh.shape["col"]
    split = Mesh(mesh.devices.reshape(rows // 2, 2, cols), (*ROW, "col"))
    in_specs = (P("col", ROW), P("col", ROW), P(ROW, "col"), P(ROW, "col"), P("col", ROW))
    out_specs = (P("col", ROW), P(ROW, "col"), P(ROW, "col"), P("col", ROW))

    def step(*arrays):
        return on_device(rows, cols, *arrays)

    return jax.shard_map(
        step, mesh=split, in_specs=in_specs, out_specs=out_specs, check_vma=False
    )
```

time: 120 us -> 121 us (level)
  matrix products: 3.36 us -> 0 us
  Pallas kernels: 1.91 us -> 4.57 us
  waiting for transfers between devices: 5.53 us -> 7.22 us
    dot_general x3 -> x0, matrix products: 3.36 us -> none  [contract(): lax.dot_general(left, right, (((left_dim,), (right_dim,)), ((), ())), pre...]
    pallas_call x1 -> x4, Pallas kernels: 0.6 us -> 3.12 us  [the longest x1 1.68 us: weight_grads(): pl.pallas_call(grad_kernel, out_shape=[jax.ShapeDtypeStruct((width, depth...]
    all_to_all x1, waiting for transfers between devices: 5.53 us -> 7.22 us  [exchange(): lax.all_to_all(array.reshape(pieces, -1, array.shape[-1]), axis, 0, 0)]
  transfers between devices with their start and end apart: 1 -> 1, of which waited for: 1 -> 1; matrix products, arithmetic and copies ran while one was open for 3% -> 0% of each run, Pallas kernels for 0% -> 1%
where the time goes in v5:
time: 121 us; the launch traced here: 120 us
  blocking collectives  92 us (76%)
  starting transfers between devices  14.8 us (12%)
  waiting for transfers between devices  7.22 us (6%)
  Pallas kernels  4.57 us (4%)
    all_gather x1, blocking collectives, on_device(): pieces = lax.all_gather(payload, ROW, axis=0, tiled=True)  31.6 us
    all_to_all x1, blocking collectives, exchange(): lax.all_to_all(array.reshape(pieces, -1, array.shape[-1]), axis, 0, 0)  28.9 us
    all_to_all x1, blocking collectives, spread(): return lax.all_to_all(copies, axis, 0, 0).reshape(-1, block.shape[1])  21.2 us
    all_to_all x1, starting transfers between devices, exchange(): lax.all_to_all(array.reshape(pieces, -1, array.shape[-1]), axis, 0, 0)  14.8 us
    all_gather x1, blocking collectives, fold(): lax.all_gather(sent.astype(jnp.float16), 'pair', axis=0).astype(jnp.float32)  10.2 us
    all_to_all x1, waiting for transfers between devices, exchange(): lax.all_to_all(array.reshape(pieces, -1, array.shape[-1]), axis, 0, 0)  7.22 us
  transfers between devices with their start and end apart: 1, of which 1 were waited for; matrix products, arithmetic and copies ran while one was open for 0% of the time, Pallas kernels for 1%

profile of v5, /device:TPU:1, one launch (start us, length us, event | category | flops | bytes accessed | tf_op | source)
XLA Modules:
  0.0 120.3 jit_solution(6669635783161935900)
XLA Ops:
  0.6 0.0 copy-start.2
  0.6 0.0 copy-start.1
  0.7 0.0 copy-start
  0.7 0.8 pad_maximum_fusion
  1.5 0.1 broadcast_in_dim.2
  1.5 21.2 %all_to_all.15 = bf16[32,8,1024]{2,1,0:T(8,128)(2,1)S(1)} all-to-all(bf16[32,8,1024]{2,1,0:T(8,128)(2,1)S(1)} %broadcast_in_dim.2), channel_id=1, replica_groups=mesh['far'=8,'pair'=2,'col'=32] {'col'}, dimensions={0} | all-to-all | bytes 1048576 | tf_op jit(solution)/shard_map/all_to_all | solution.py:39
  22.7 0.0 copy-done.2
  22.7 0.0 copy-done.1
  22.7 0.0 copy-done
  22.7 0.6 partial_sums.1
  23.4 10.2 %all-gather = f16[256,1408]{1,0:T(8,128)(2,1)S(1)} all-gather(f16[128,1408]{1,0:T(8,128)(2,1)S(1)} %convert_element_type.12), channel_id=2, replica_groups=mesh['far'=8,'pair'=2,'col'=32] {'pair'}, dimensions={0}, use_global_device_ids=true | all-gather | bytes 1081344 | tf_op jit(solution)/shard_map/all_gather | solution.py:101
  33.6 0.1 convert.got
  33.7 0.3 fold.1
  34.0 28.9 %all_to_all.16 = f16[16,8,1408]{2,1,0:T(8,128)(2,1)S(1)} all-to-all(f16[16,8,1408]{2,1,0:T(8,128)(2,1)S(1)} %convert_bitcast_fusion), channel_id=1, replica_groups=mesh['far'=8,'pair'=2,'col'=32] {'far','pair'}, dimensions={0} | all-to-all | bytes 720896 | tf_op jit(solution)/shard_map/all_to_all | solution.py:34
  63.0 0.2 activations.1
  63.2 31.6 %all_gather.11.pieces = bf16[16,8,2816]{2,1,0:T(8,128)(2,1)S(1)} all-gather(bf16[1,8,2816]{2,1,0:T(8,128)(2,1)S(1)} %activations.1), channel_id=1, replica_groups=mesh['far'=8,'pair'=2,'col'=32] {'far','pair'}, dimensions={0}, use_global_device_ids=true | all-gather | bytes 765952 | tf_op jit(solution)/shard_map/all_gather | solution.py:214
  94.8 1.2 block_inputs.1
  96.0 14.8 %all-to-all-start.2 = ((bf16[32,8,512]{2,1,0:T(8,128)(2,1)}), bf16[32,8,512]{2,1,0:T(8,128)(2,1)S(1)}, u32[]{:S(2)}, u32[]{:S(2)}) async-start(bf16[32,8,512]{2,1,0:T(8,128)(2,1)} %bitcast.6), calls=%async_computation.2 | async-start | bytes 524288 | tf_op jit(solution)/shard_map/all_to_all | solution.py:34
  110.8 1.7 %weight_grads.1 = (bf16[448,512]{1,0:T(8,128)(2,1)}, bf16[448,512]{1,0:T(8,128)(2,1)}, bf16[448,512]{1,0:T(8,128)(2,1)}) custom-call(bf16[16,2,8,1024]{3,2,1,0:T(8,128)(2,1)S(1)} %bitcast.13, bf16[16,8,2816]{2,1,0:T(8,128)(2,1)S(1)} %all_gather.11.pieces), custom_call_target="tpu_custom_call" | custom-call | flops 352321536 | bytes 4194304 | tf_op jit(solution)/shard_map/weight_grads/pallas_call | solution.py:182
  112.5 7.2 %all-to-all-done.2.blocks = bf16[32,8,512]{2,1,0:T(8,128)(2,1)S(1)} async-done(((bf16[32,8,512]{2,1,0:T(8,128)(2,1)}), bf16[32,8,512]{2,1,0:T(8,128)(2,1)S(1)}, u32[]{:S(2)}, u32[]{:S(2)}) %all-to-all-start.2) | async-done | bytes 262176 | tf_op jit(solution)/shard_map/all_to_all | solution.py:34
  119.7 0.6 final_sum.1
  (3 shorter events, 0.1 us)
Async XLA Ops:
  0.6 22.1 %copy-start.2 = (bf16[448,512]{1,0:T(8,128)(2,1)S(1)}, bf16[448,512]{1,0:T(8,128)(2,1)}, u32[]{:S(2)}) copy-start(bf16[448,512]{1,0:T(8,128)(2,1)} %w_down.1) | copy-start | bytes 1376260
  0.6 22.1 %copy-start.1 = (bf16[512,448]{0,1:T(8,128)(2,1)S(1)}, bf16[512,448]{0,1:T(8,128)(2,1)}, u32[]{:S(2)}) copy-start(bf16[512,448]{0,1:T(8,128)(2,1)} %param.8) | copy-start | bytes 1376260
  0.7 22.1 %copy-start = (bf16[512,448]{0,1:T(8,128)(2,1)S(1)}, bf16[512,448]{0,1:T(8,128)(2,1)}, u32[]{:S(2)}) copy-start(bf16[512,448]{0,1:T(8,128)(2,1)} %param.7) | copy-start | bytes 1376260
  96.0 23.7 %all-to-all-start.2 = ((bf16[32,8,512]{2,1,0:T(8,128)(2,1)}), bf16[32,8,512]{2,1,0:T(8,128)(2,1)S(1)}, u32[]{:S(2)}, u32[]{:S(2)}) async-start(bf16[32,8,512]{2,1,0:T(8,128)(2,1)} %bitcast.6), calls=%async_computation.2 | async-start | bytes 524288 | tf_op jit(solution)/shard_map/all_to_all | solution.py:34

commit v6 on v5

--- a/solution.py
+++ b/solution.py
@@ -7,6 +7,8 @@
 from jax.sharding import PartitionSpec as P
 
 ROW = ("far", "pair")
+COL = ("chip", "core")
+SWAP = [(0, 1), (1, 0)]
 LEAST = -100.0
 SHIFT = 9.0
 PAIR_SHIFT = 8.0
@@ -34,16 +36,12 @@
     return lax.all_to_all(array.reshape(pieces, -1, array.shape[-1]), axis, 0, 0)
 
 
-def spread(block, axis, pieces):
-    copies = jnp.broadcast_to(block[None], (pieces, *block.shape))
-    return lax.all_to_all(copies, axis, 0, 0).reshape(-1, block.shape[1])
-
-
-def partial_kernel(both, w_gate, w_up, w_down, sent, kept):
-    width, depth = w_gate.shape
-    mine = lax.axis_index("pair") == 0
+def partial_kernel(both, *refs):
+    own, theirs, sent, kept = refs
+    width, depth = own.shape[0] // 3, own.shape[1]
+    same = lax.axis_index("pair") == lax.axis_index("core")
     notes = []
-    for i, (w, side) in enumerate(((w_gate, 0), (w_up, 0), (w_down, 1))):
+    for i, side in enumerate((0, 0, 1)):
         x = both[:, side * depth : (side + 1) * depth]
         if i != 1:
             largest = jnp.max(jnp.abs(x).astype(jnp.float32), axis=0, keepdims=True)
@@ -51,27 +49,26 @@
             exp = jnp.ceil(jnp.log2(jnp.maximum(largest, 2.0**LEAST)))
             scale = jnp.exp2(SHIFT - exp)
             notes.append(jnp.broadcast_to(exp, (sent.shape[0], NOTE // 2)))
-        part = contract(x, w[...], 1, 1).reshape(-1, 2, 8, width)
-        even = part[:, 0].reshape(-1, width)
-        odd = part[:, 1].reshape(-1, width)
-        at = pl.ds(i * width, width)
-        kept[:, at] = jnp.where(mine, even, odd)
-        sent[:, at] = jnp.where(mine, odd, even) * scale
+        at = slice(i * width, (i + 1) * width)
+        first = contract(x, own[at], 1, 1)
+        second = contract(x, theirs[at], 1, 1)
+        kept[:, at] = jnp.where(same, first, second)
+        sent[:, at] = jnp.where(same, second, first) * scale
     notes = jnp.concatenate(notes, axis=1)
     kept[:, 3 * width :] = notes
     sent[:, 3 * width :] = notes
 
 
-def partial_sums(both, w_gate, w_up, w_down):
-    tokens, width = both.shape[0], w_gate.shape[0]
+def partial_sums(both, own, theirs):
+    tokens, width = both.shape[0], own.shape[0] // 3
     return pl.pallas_call(
         partial_kernel,
-        out_shape=[jax.ShapeDtypeStruct((tokens // 2, 3 * width + NOTE), jnp.float32)] * 2,
-        in_specs=[pl.BlockSpec(memory_space=pltpu.VMEM)] * 4,
+        out_shape=[jax.ShapeDtypeStruct((tokens, 3 * width + NOTE), jnp.float32)] * 2,
+        in_specs=[pl.BlockSpec(memory_space=pltpu.VMEM)] * 3,
         out_specs=[pl.BlockSpec(memory_space=pltpu.VMEM)] * 2,
         compiler_params=pltpu.CompilerParams(vmem_limit_bytes=16 << 20),
         name="partial_sums",
-    )(both, w_gate, w_up, w_down)
+    )(both, own, theirs)
 
 
 def exponents(block):
@@ -138,56 +135,80 @@
     )(blocks)
 
 
-def piece(pieces, h, which, width):
+def piece(pieces, which, width):
+    return pieces[:, :, which * width : (which + 1) * width].reshape(-1, width)
+
+
+def of_core(pieces, core):
     stride = pieces.shape[2] // 2
-    at = h * stride + which * width
-    return pieces[:, :, at : at + width].reshape(-1, width)
-
-
-def block_kernel(pieces, w_gate, w_up, out):
-    width = w_gate.shape[0]
-    for h in range(2):
-        total = contract(piece(pieces, h, 0, width), w_gate[...], 1, 0)
-        total += contract(piece(pieces, h, 1, width), w_up[...], 1, 0)
-        out[:, h] = total.reshape(out.shape[0], *out.shape[2:]).astype(out.dtype)
-
-
-def block_inputs(pieces, w_gate, w_up):
+    return pieces[:, :, pl.ds(pl.multiple_of(core * stride, 128), stride)]
+
+
+def block_kernel(pieces, own, theirs, out):
+    width = own.shape[0] // 3
+    core = lax.axis_index("core")
+    total = 0.0
+    for c, weights in ((core, own), (1 - core, theirs)):
+        part = of_core(pieces, c)
+        total += contract(piece(part, 0, width), weights[:width], 1, 0)
+        total += contract(piece(part, 1, width), weights[width : 2 * width], 1, 0)
+    out[...] = total.astype(out.dtype)
+
+
+def block_inputs(pieces, own, theirs):
     return pl.pallas_call(
         block_kernel,
         out_shape=jax.ShapeDtypeStruct(
-            (pieces.shape[0], 2, pieces.shape[1], w_gate.shape[1]), jnp.bfloat16
+            (pieces.shape[0] * pieces.shape[1], own.shape[1]), jnp.bfloat16
         ),
         in_specs=[pl.BlockSpec(memory_space=pltpu.VMEM)] * 3,
         out_specs=pl.BlockSpec(memory_space=pltpu.VMEM),
         compiler_params=pltpu.CompilerParams(vmem_limit_bytes=16 << 20),
         name="block_inputs",
-    )(pieces, w_gate, w_up)
-
-
-def grad_kernel(both, pieces, grad_gate, grad_up, grad_down):
+    )(pieces, own, theirs)
+
+
+def give_kernel(pieces, out):
+    out[...] = of_core(pieces, 1 - lax.axis_index("core")).reshape(out.shape)
+
+
+def given(pieces):
+    shape = (pieces.shape[0] * pieces.shape[1], pieces.shape[2] // 2)
+    return pl.pallas_call(
+        give_kernel,
+        out_shape=jax.ShapeDtypeStruct(shape, jnp.bfloat16),
+        in_specs=[pl.BlockSpec(memory_space=pltpu.VMEM)],
+        out_specs=pl.BlockSpec(memory_space=pltpu.VMEM),
+        compiler_params=pltpu.CompilerParams(vmem_limit_bytes=16 << 20),
+        name="given",
+    )(pieces)
+
+
+def grad_kernel(both, pieces, got, grad_gate, grad_up, grad_down):
     width, depth = grad_gate.shape
+    core = lax.axis_index("core")
+    mine = of_core(pieces, core)
     for which, side, out in ((0, 0, grad_gate), (1, 0, grad_up), (2, 1, grad_down)):
-        total = None
-        for h in range(2):
-            x = both[:, h, :, side * depth : (side + 1) * depth].reshape(-1, depth)
-            term = contract(piece(pieces, h, which, width), x, 0, 0)
-            total = term if total is None else total + term
+        units = slice(which * width, (which + 1) * width)
+        features = slice(side * depth, (side + 1) * depth)
+        total = contract(piece(mine, which, width), both[core, :, features], 0, 0)
+        total += contract(got[1 - core, :, units], both[1 - core, :, features], 0, 0)
         out[...] = total.astype(out.dtype)
 
 
-def weight_grads(both, pieces, width):
-    depth = both.shape[1] // 2
-    both = both.reshape(pieces.shape[0], 2, pieces.shape[1], 2 * depth)
+def weight_grads(both, pieces, got, width):
+    depth = both.shape[2] // 2
     return pl.pallas_call(
         grad_kernel,
         out_shape=[jax.ShapeDtypeStruct((width, depth), jnp.bfloat16)] * 3,
-        in_specs=[pl.BlockSpec(memory_space=pltpu.VMEM)] * 2,
+        in_specs=[pl.BlockSpec(memory_space=pltpu.VMEM)] * 3,
         out_specs=[pl.BlockSpec(memory_space=pltpu.VMEM)] * 3,
         compiler_params=pltpu.CompilerParams(vmem_limit_bytes=16 << 20),
-        cost_estimate=pl.CostEstimate(flops=6 * 256 * 448 * 512, bytes_accessed=4 << 20, transcendentals=0),
+        cost_estimate=pl.CostEstimate(
+            flops=24 * both.shape[1] * width * depth, bytes_accessed=4 << 20, transcendentals=0
+        ),
         name="weight_grads",
-    )(both, pieces)
+    )(both, pieces, got)
 
 
 def sum_kernel(blocks, out):
@@ -205,28 +226,35 @@
     )(blocks)
 
 
-def on_device(rows, cols, inputs, out_grad, w_gate, w_up, w_down):
+def on_device(rows, chips, inputs, out_grad, w_gate, w_up, w_down):
     width = w_gate.shape[1]
-    both = spread(jnp.concatenate([inputs, out_grad], axis=1), "col", cols)
-    partial = fold(*partial_sums(both, w_gate.T, w_up.T, w_down))
-    blocks = exchange(partial.astype(jnp.float16), ROW, rows).astype(jnp.float32)
-    payload = activations(blocks)
+    own = jnp.concatenate([w_gate.T, w_up.T, w_down], axis=0)
+    copies = jnp.concatenate([inputs, out_grad], axis=1)
+    copies = jnp.broadcast_to(copies[None], (chips, *copies.shape))
+    both = lax.all_to_all(copies, "chip", 0, 0).reshape(-1, copies.shape[2])
+    theirs = lax.ppermute(own, "core", SWAP)
+    partial = fold(*partial_sums(both, own, theirs))
+    blocks = exchange(partial.astype(jnp.float16), ROW, rows)
+    payload = activations(blocks.astype(jnp.float32))
     pieces = lax.all_gather(payload, ROW, axis=0, tiled=True)
-    block_in = block_inputs(pieces, w_gate.T, w_up.T).reshape(both.shape[0], -1)
+    block_in = block_inputs(pieces, own, theirs)
     block_in, pieces = lax.optimization_barrier((block_in, pieces))
-    grad_inputs = final_sum(exchange(block_in, "col", cols))
-    grad_gate, grad_up, grad_down = weight_grads(both, pieces, width)
+    block_in = exchange(block_in, "chip", chips)
+    got = lax.all_gather(given(pieces), "core", axis=0)
+    grads = weight_grads(lax.all_gather(both, "core", axis=0), pieces, got, width)
+    block_in, grad_gate, grad_up, grad_down = lax.optimization_barrier((block_in, *grads))
+    grad_inputs = final_sum(block_in)
     return (grad_inputs, grad_gate.T, grad_up.T, grad_down)
 
 
 def solution(mesh):
     rows, cols = mesh.shape["row"], mesh.shape["col"]
-    split = Mesh(mesh.devices.reshape(rows // 2, 2, cols), (*ROW, "col"))
-    in_specs = (P("col", ROW), P("col", ROW), P(ROW, "col"), P(ROW, "col"), P("col", ROW))
-    out_specs = (P("col", ROW), P(ROW, "col"), P(ROW, "col"), P("col", ROW))
+    split = Mesh(mesh.devices.reshape(rows // 2, 2, cols // 2, 2), ROW + COL)
+    in_specs = (P(COL, ROW), P(COL, ROW), P(ROW, COL), P(ROW, COL), P(COL, ROW))
+    out_specs = (P(COL, ROW), P(ROW, COL), P(ROW, COL), P(COL, ROW))
 
     def step(*arrays):
-        return on_device(rows, cols, *arrays)
+        return on_device(rows, cols // 2, *arrays)
 
     return jax.shard_map(
         step, mesh=split, in_specs=in_specs, out_specs=out_specs, check_vma=False

time: 121 us -> 115 us (0.950); the launches traced: 120 us -> 112 us
  blocking collectives: 92 us -> 66.9 us
  starting transfers between devices: 14.8 us -> 25.7 us
  waiting for transfers between devices: 7.22 us -> 11.7 us
  other arithmetic: 1.04 us -> 2.36 us
    all_to_all x2 -> x1, blocking collectives: 50.1 us -> 11.1 us  [on_device(): both = lax.all_to_all(copies, 'chip', 0, 0).reshape(-1, copies.shape[2])]
    all_gather x0 -> x2, blocking collectives: none -> 16.6 us  [the longest x1 12.4 us: on_device(): got = lax.all_gather(given(pieces), 'core', axis=0)]
    ppermute x0 -> x1, starting transfers between devices: none -> 8.79 us  [on_device(): theirs = lax.ppermute(own, 'core', SWAP)]
    all_to_all x1 -> x2, waiting for transfers between devices: 7.22 us -> 11.7 us  [exchange(): lax.all_to_all(array.reshape(pieces, -1, array.shape[-1]), axis, 0, 0)]
    all_to_all x1 -> x2, starting transfers between devices: 14.8 us -> 17 us  [exchange(): lax.all_to_all(array.reshape(pieces, -1, array.shape[-1]), axis, 0, 0)]
    all_gather x1, blocking collectives: 31.6 us -> 29.6 us  [on_device(): pieces = lax.all_gather(payload, ROW, axis=0, tiled=True)]
  transfers between devices with their start and end apart: 1 -> 3, of which waited for: 1 -> 1; matrix products, arithmetic and copies ran while one was open for 0% -> 0% of each run, Pallas kernels for 1% -> 2%
where the time goes in v6:
time: 115 us; the launch traced here: 112 us
  blocking collectives  66.9 us (58%)
  starting transfers between devices  25.7 us (22%)
  waiting for transfers between devices  11.7 us (10%)
  Pallas kernels  4.26 us (4%)
  other arithmetic  2.36 us (2%)
    all_gather x1, blocking collectives, on_device(): pieces = lax.all_gather(payload, ROW, axis=0, tiled=True)  29.6 us
    all_to_all x2, starting transfers between devices, exchange(): lax.all_to_all(array.reshape(pieces, -1, array.shape[-1]), axis, 0, 0)  17 us
    all_gather x1, blocking collectives, on_device(): got = lax.all_gather(given(pieces), 'core', axis=0)  12.4 us
    all_to_all x2, waiting for transfers between devices, exchange(): lax.all_to_all(array.reshape(pieces, -1, array.shape[-1]), axis, 0, 0)  11.7 us
    all_to_all x1, blocking collectives, on_device(): both = lax.all_to_all(copies, 'chip', 0, 0).reshape(-1, copies.shape[2])  11.1 us
    all_gather x1, blocking collectives, fold(): lax.all_gather(sent.astype(jnp.float16), 'pair', axis=0).astype(jnp.float32)  9.5 us
    ppermute x1, starting transfers between devices, on_device(): theirs = lax.ppermute(own, 'core', SWAP)  8.79 us
    all_gather x1, blocking collectives, on_device(): lax.all_gather(both, 'core', axis=0)  4.26 us
  transfers between devices with their start and end apart: 3, of which 1 were waited for; matrix products, arithmetic and copies ran while one was open for 0% of the time, Pallas kernels for 2%

profile of v6, /device:TPU:1, one launch (start us, length us, event | category | flops | bytes accessed | tf_op | source)
XLA Modules:
  0.0 112.4 jit_solution(7768298986492253012)
XLA Ops:
  0.7 1.4 %pad_maximum_fusion.refs_0_.own = bf16[1344,512]{1,0:T(8,128)(2,1)S(1)} fusion(bf16[448,512]{1,0:T(8,128)(2,1)} %param.9, bf16[448,512]{1,0:T(8,128)(2,1)} %bitcast.17, bf16[448,512]{1,0:T(8,128)(2,1)} %bitcast.18), kind=kLoop, calls=%fused_computation | loop fusion | flops 4128768 | bytes 2752512 | tf_op jit(solution)/shard_map/concatenate | solution.py:231
  2.1 8.8 %collective-permute-start = (bf16[1344,512]{1,0:T(8,128)(2,1)S(1)}, bf16[1344,512]{1,0:T(8,128)(2,1)S(1)}, u32[]{:S(2)}, u32[]{:S(2)}) collective-permute-start(bf16[1344,512]{1,0:T(8,128)(2,1)S(1)} %pad_maximum_fusion.refs_0_.own), channel_id=1, source_target_pairs={{0,1},{1,0},{2,3},{3,2},{4,5},{5,4},{6,7},{7,6},{8,9},{9,8},{10,11... | collective-permute-start | bytes 4128776 | tf_op jit(solution)/shard_map/ppermute | solution.py:235
  10.9 11.1 %all_to_all.15 = bf16[16,8,1024]{2,1,0:T(8,128)(2,1)S(1)} all-to-all(bf16[16,8,1024]{2,1,0:T(8,128)(2,1)S(1)} %broadcast_in_dim.2), channel_id=1, replica_groups=mesh['far'=8,'pair'=2,'chip'=16,'core'=2] {'chip'}, dimensions={0} | all-to-all | bytes 524288 | tf_op jit(solution)/shard_map/all_to_all | solution.py:234
  22.0 0.0 collective-permute-done.refs_1_.theirs
  22.1 0.9 partial_sums.1
  23.1 9.5 %all-gather = f16[256,1408]{1,0:T(8,128)(2,1)S(1)} all-gather(f16[128,1408]{1,0:T(8,128)(2,1)S(1)} %convert_element_type.12), channel_id=2, replica_groups=mesh['far'=8,'pair'=2,'chip'=16,'core'=2] {'pair'}, dimensions={0}, use_global_device_ids=true | all-gather | bytes 1081344 | tf_op jit(solution)/shard_map/all_gather | solution.py:98
  32.6 0.1 convert.got
  32.7 0.3 fold.1
  32.9 0.8 convert_bitcast_fusion
  33.7 13.4 %all-to-all-start.1 = ((f16[16,8,1408]{2,1,0:T(8,128)(2,1)}), f16[16,8,1408]{2,1,0:T(8,128)(2,1)S(1)}, u32[]{:S(2)}, u32[]{:S(2)}) async-start(f16[16,8,1408]{2,1,0:T(8,128)(2,1)} %convert_bitcast_fusion), calls=%async_computation.1 | async-start | bytes 720896 | tf_op jit(solution)/shard_map/all_to_all | solution.py:36
  47.2 4.3 %all_gather.21.both = bf16[2,128,1024]{2,1,0:T(8,128)(2,1)} all-gather(bf16[1,128,1024]{2,1,0:T(8,128)(2,1)S(1)} %bitcast.13), channel_id=1, replica_groups=mesh['far'=8,'pair'=2,'chip'=16,'core'=2] {'core'}, dimensions={0}, use_global_device_ids=true | all-gather | bytes 786432 | tf_op jit(solution)/shard_map/all_gather | solution.py:244
  51.4 11.7 %all-to-all-done.1 = f16[16,8,1408]{2,1,0:T(8,128)(2,1)S(1)} async-done(((f16[16,8,1408]{2,1,0:T(8,128)(2,1)}), f16[16,8,1408]{2,1,0:T(8,128)(2,1)S(1)}, u32[]{:S(2)}, u32[]{:S(2)}) %all-to-all-start.1) | async-done | bytes 360480 | tf_op jit(solution)/shard_map/all_to_all | solution.py:36
  63.2 0.2 activations.1
  63.4 29.6 %all_gather.20.pieces = bf16[16,8,2816]{2,1,0:T(8,128)(2,1)S(1)} all-gather(bf16[1,8,2816]{2,1,0:T(8,128)(2,1)S(1)} %activations.1), channel_id=1, replica_groups=mesh['far'=8,'pair'=2,'chip'=16,'core'=2] {'far','pair'}, dimensions={0}, use_global_device_ids=true | all-gather | bytes 765952 | tf_op jit(solution)/shard_map/all_gather | solution.py:239
  93.0 0.5 block_inputs.1
  93.5 0.0 copy-start
  93.5 0.0 copy-start.1
  93.6 0.6 copy-done
  94.2 3.5 %all-to-all-start.2 = ((bf16[16,8,512]{2,1,0:T(8,128)(2,1)}), bf16[16,8,512]{2,1,0:T(8,128)(2,1)S(1)}, u32[]{:S(2)}, u32[]{:S(2)}) async-start(bf16[16,8,512]{2,1,0:T(8,128)(2,1)} %bitcast.15), calls=%async_computation.2 | async-start | bytes 262144 | tf_op jit(solution)/shard_map/all_to_all | solution.py:36
  97.7 12.4 %all-gather.1 = bf16[256,1408]{1,0:T(8,128)(2,1)S(1)} all-gather(bf16[128,1408]{1,0:T(8,128)(2,1)S(1)} %given.1), channel_id=3, replica_groups=mesh['far'=8,'pair'=2,'chip'=16,'core'=2] {'core'}, dimensions={0}, use_global_device_ids=true | all-gather | bytes 1081344 | tf_op jit(solution)/shard_map/all_gather | solution.py:243
  110.1 0.0 copy-done.1
  110.1 1.7 %weight_grads.1 = (bf16[448,512]{1,0:T(8,128)(2,1)}, bf16[448,512]{1,0:T(8,128)(2,1)}, bf16[448,512]{1,0:T(8,128)(2,1)}) custom-call(bf16[2,128,1024]{2,1,0:T(8,128)(2,1)S(1)} %copy-done.1, bf16[16,8,2816]{2,1,0:T(8,128)(2,1)S(1)} %all_gather.20.pieces, bf16[2,128,1408]{2,1,0:T(8,128)(2,1)S(1)} %bitcast.14), custom_call_target="tpu_custom_call" | custom-call | flops 704643072 | bytes 4194304 | tf_op jit(solution)/shard_map/weight_grads/pallas_call | solution.py:201
  111.8 0.0 all-to-all-done.2.blocks
  111.8 0.6 final_sum.1
  (9 shorter events, 0.2 us)
Async XLA Ops:
  0.6 10.2 %copy-start.3 = (bf16[8,512]{1,0:T(8,128)(2,1)S(1)}, bf16[8,512]{1,0:T(8,128)(2,1)}, u32[]{:S(2)}) copy-start(bf16[8,512]{1,0:T(8,128)(2,1)} %param.5) | copy-start | bytes 24580
  0.6 10.2 %copy-start.2 = (bf16[8,512]{1,0:T(8,128)(2,1)S(1)}, bf16[8,512]{1,0:T(8,128)(2,1)}, u32[]{:S(2)}) copy-start(bf16[8,512]{1,0:T(8,128)(2,1)} %param.6) | copy-start | bytes 24580
  2.1 20.0 %collective-permute-start = (bf16[1344,512]{1,0:T(8,128)(2,1)S(1)}, bf16[1344,512]{1,0:T(8,128)(2,1)S(1)}, u32[]{:S(2)}, u32[]{:S(2)}) collective-permute-start(bf16[1344,512]{1,0:T(8,128)(2,1)S(1)} %pad_maximum_fusion.refs_0_.own), channel_id=1, source_target_pairs={{0,1},{1,0},{2,3},{3,2},{4,5},{5,4},{6,7},{7,6},{8,9},{9,8},{10,11... | collective-permute-start | bytes 4128776 | tf_op jit(solution)/shard_map/ppermute | solution.py:235
  33.7 29.4 %all-to-all-start.1 = ((f16[16,8,1408]{2,1,0:T(8,128)(2,1)}), f16[16,8,1408]{2,1,0:T(8,128)(2,1)S(1)}, u32[]{:S(2)}, u32[]{:S(2)}) async-start(f16[16,8,1408]{2,1,0:T(8,128)(2,1)} %convert_bitcast_fusion), calls=%async_computation.1 | async-start | bytes 720896 | tf_op jit(solution)/shard_map/all_to_all | solution.py:36
  93.5 0.6 copy-start
  93.5 16.5 %copy-start.1 = (bf16[2,128,1024]{2,1,0:T(8,128)(2,1)S(1)}, bf16[2,128,1024]{2,1,0:T(8,128)(2,1)}, u32[]{:S(2)}) copy-start(bf16[2,128,1024]{2,1,0:T(8,128)(2,1)} %all_gather.21.both) | copy-start | bytes 1572868
  94.2 17.6 %all-to-all-start.2 = ((bf16[16,8,512]{2,1,0:T(8,128)(2,1)}), bf16[16,8,512]{2,1,0:T(8,128)(2,1)S(1)}, u32[]{:S(2)}, u32[]{:S(2)}) async-start(bf16[16,8,512]{2,1,0:T(8,128)(2,1)} %bitcast.15), calls=%async_computation.2 | async-start | bytes 262144 | tf_op jit(solution)/shard_map/all_to_all | solution.py:36

commit v7 on v6

--- a/solution.py
+++ b/solution.py
@@ -77,7 +77,8 @@
 
 
 def fold_kernel(got, kept, out):
-    theirs, mine = got[1 - lax.axis_index("pair")], kept[...]
+    parity, core = lax.axis_index("pair"), lax.axis_index("core")
+    theirs, mine = got[jnp.where(core == 0, 1 - parity, parity)], kept[...]
     at = mine.shape[1] - NOTE
     column = lax.broadcasted_iota(jnp.int32, (mine.shape[0], at), 1)
     grads = column >= 2 * (at // 3)
@@ -94,8 +95,16 @@
     )
 
 
-def fold(sent, kept):
-    got = lax.all_gather(sent.astype(jnp.float16), "pair", axis=0).astype(jnp.float32)
+def neighbours(rows):
+    return [(2 * z + c, 2 * ((z + (1 if z % 2 == c else -1)) % rows) + c) for z in range(rows) for c in range(2)]
+
+
+def fold(sent, kept, rows):
+    groups = sorted({tuple(sorted(p, key=lambda i: (i - (i % 2) * 2) % (2 * rows))) for p in neighbours(rows)})
+    got = lax.all_gather(
+        sent.astype(jnp.float16), (*ROW, "core"), axis=0, axis_index_groups=[list(g) for g in groups]
+    )
+    got = got.astype(jnp.float32)
     return pl.pallas_call(
         fold_kernel,
         out_shape=jax.ShapeDtypeStruct(kept.shape, jnp.float32),
@@ -184,16 +193,22 @@
     )(pieces)
 
 
-def grad_kernel(both, pieces, got, grad_gate, grad_up, grad_down):
-    width, depth = grad_gate.shape
+def grad_kernel(both, pieces, got, *refs):
+    outs, (hold, sems) = refs[:3], refs[3:]
+    width, depth = outs[0].shape
     core = lax.axis_index("core")
     mine = of_core(pieces, core)
-    for which, side, out in ((0, 0, grad_gate), (1, 0, grad_up), (2, 1, grad_down)):
+    stores = []
+    for which, side in ((2, 1), (0, 0), (1, 0)):
         units = slice(which * width, (which + 1) * width)
         features = slice(side * depth, (side + 1) * depth)
         total = contract(piece(mine, which, width), both[core, :, features], 0, 0)
         total += contract(got[1 - core, :, units], both[1 - core, :, features], 0, 0)
-        out[...] = total.astype(out.dtype)
+        hold[which] = total.astype(hold.dtype)
+        stores.append(pltpu.make_async_copy(hold.at[which], outs[which], sems.at[which]))
+        stores[-1].start()
+    for store in stores:
+        store.wait()
 
 
 def weight_grads(both, pieces, got, width):
@@ -202,7 +217,11 @@
         grad_kernel,
         out_shape=[jax.ShapeDtypeStruct((width, depth), jnp.bfloat16)] * 3,
         in_specs=[pl.BlockSpec(memory_space=pltpu.VMEM)] * 3,
-        out_specs=[pl.BlockSpec(memory_space=pltpu.VMEM)] * 3,
+        out_specs=[pl.BlockSpec(memory_space=pl.ANY)] * 3,
+        scratch_shapes=[
+            pltpu.VMEM((3, width, depth), jnp.bfloat16),
+            pltpu.SemaphoreType.DMA((3,)),
+        ],
         compiler_params=pltpu.CompilerParams(vmem_limit_bytes=16 << 20),
         cost_estimate=pl.CostEstimate(
             flops=24 * both.shape[1] * width * depth, bytes_accessed=4 << 20, transcendentals=0
@@ -233,12 +252,12 @@
     copies = jnp.broadcast_to(copies[None], (chips, *copies.shape))
     both = lax.all_to_all(copies, "chip", 0, 0).reshape(-1, copies.shape[2])
     theirs = lax.ppermute(own, "core", SWAP)
-    partial = fold(*partial_sums(both, own, theirs))
+    partial = fold(*partial_sums(both, own, theirs), rows)
     blocks = exchange(partial.astype(jnp.float16), ROW, rows)
     payload = activations(blocks.astype(jnp.float32))
     pieces = lax.all_gather(payload, ROW, axis=0, tiled=True)
     block_in = block_inputs(pieces, own, theirs)
-    block_in, pieces = lax.optimization_barrier((block_in, pieces))
+    block_in, pieces, both = lax.optimization_barrier((block_in, pieces, both))
     block_in = exchange(block_in, "chip", chips)
     got = lax.all_gather(given(pieces), "core", axis=0)
     grads = weight_grads(lax.all_gather(both, "core", axis=0), pieces, got, width)

time: 115 us -> 114 us (level); the launches traced: 112 us -> 113 us
  blocking collectives: 66.9 us -> 93.8 us
  starting transfers between devices: 25.7 us -> 12.3 us
  waiting for transfers between devices: 11.7 us -> 0.01 us
    all_to_all x0 -> x1, blocking collectives: none -> 23.9 us  [exchange(): lax.all_to_all(array.reshape(pieces, -1, array.shape[-1]), axis, 0, 0)]
    all_to_all x2 -> x1, starting transfers between devices: 17 us -> 3.51 us  [exchange(): lax.all_to_all(array.reshape(pieces, -1, array.shape[-1]), axis, 0, 0)]
    all_to_all x2 -> x1, waiting for transfers between devices: 11.7 us -> 0.01 us  [exchange(): lax.all_to_all(array.reshape(pieces, -1, array.shape[-1]), axis, 0, 0)]
    all_gather x1, blocking collectives: 9.5 us -> 13.3 us  [fold(): lax.all_gather(sent.astype(jnp.float16), (*ROW, 'core'), axis=0, axis_ind...]
    all_gather x1, blocking collectives: 4.26 us -> 2.17 us  [on_device(): lax.all_gather(both, 'core', axis=0)]
    all_gather x1, blocking collectives: 29.6 us -> 31.1 us  [on_device(): pieces = lax.all_gather(payload, ROW, axis=0, tiled=True)]
  transfers between devices with their start and end apart: 3 -> 2, of which waited for: 1 -> 0; matrix products, arithmetic and copies ran while one was open for 0% -> 0% of each run, Pallas kernels for 2% -> 2%
where the time goes in v7:
time: 114 us; the launch traced here: 113 us
  blocking collectives  93.8 us (82%)
  starting transfers between devices  12.3 us (11%)
  Pallas kernels  4.96 us (4%)
  other arithmetic  1.62 us (1%)
    all_gather x1, blocking collectives, on_device(): pieces = lax.all_gather(payload, ROW, axis=0, tiled=True)  31.1 us
    all_to_all x1, blocking collectives, exchange(): lax.all_to_all(array.reshape(pieces, -1, array.shape[-1]), axis, 0, 0)  23.9 us
    all_gather x1, blocking collectives, fold(): lax.all_gather(sent.astype(jnp.float16), (*ROW, 'core'), axis=0, axis_ind...  13.3 us
    all_gather x1, blocking collectives, on_device(): got = lax.all_gather(given(pieces), 'core', axis=0)  12.3 us
    all_to_all x1, blocking collectives, on_device(): both = lax.all_to_all(copies, 'chip', 0, 0).reshape(-1, copies.shape[2])  11.1 us
    ppermute x1, starting transfers between devices, on_device(): theirs = lax.ppermute(own, 'core', SWAP)  8.79 us
    all_to_all x1, starting transfers between devices, exchange(): lax.all_to_all(array.reshape(pieces, -1, array.shape[-1]), axis, 0, 0)  3.51 us
  transfers between devices with their start and end apart: 2, of which 0 were waited for; matrix products, arithmetic and copies ran while one was open for 0% of the time, Pallas kernels for 2%

profile of v7, /device:TPU:1, one launch (start us, length us, event | category | flops | bytes accessed | tf_op | source)
XLA Modules:
  0.0 113.5 jit_solution(8065895413204783361)
XLA Ops:
  0.6 0.0 copy-start
  0.6 0.0 copy-start.1
  0.7 1.4 %pad_maximum_fusion.refs_0_.own = bf16[1344,512]{1,0:T(8,128)(2,1)S(1)} fusion(bf16[448,512]{1,0:T(8,128)(2,1)} %param.9, bf16[448,512]{1,0:T(8,128)(2,1)} %bitcast.17, bf16[448,512]{1,0:T(8,128)(2,1)} %bitcast.18), kind=kLoop, calls=%fused_computation | loop fusion | flops 4128768 | bytes 2752512 | tf_op jit(solution)/shard_map/concatenate | solution.py:250
  2.1 8.8 %collective-permute-start = (bf16[1344,512]{1,0:T(8,128)(2,1)S(1)}, bf16[1344,512]{1,0:T(8,128)(2,1)S(1)}, u32[]{:S(2)}, u32[]{:S(2)}) collective-permute-start(bf16[1344,512]{1,0:T(8,128)(2,1)S(1)} %pad_maximum_fusion.refs_0_.own), channel_id=1, source_target_pairs={{0,1},{1,0},{2,3},{3,2},{4,5},{5,4},{6,7},{7,6},{8,9},{9,8},{10,11... | collective-permute-start | bytes 4128776 | tf_op jit(solution)/shard_map/ppermute | solution.py:254
  10.8 0.0 copy-done
  10.9 0.0 copy-done.1
  10.9 11.1 %all_to_all.15 = bf16[16,8,1024]{2,1,0:T(8,128)(2,1)S(1)} all-to-all(bf16[16,8,1024]{2,1,0:T(8,128)(2,1)S(1)} %broadcast_in_dim.2), channel_id=1, replica_groups=mesh['far'=8,'pair'=2,'chip'=16,'core'=2] {'chip'}, dimensions={0} | all-to-all | bytes 524288 | tf_op jit(solution)/shard_map/all_to_all | solution.py:253
  22.0 0.0 collective-permute-done.refs_1_.theirs
  22.1 0.9 partial_sums.1
  23.1 13.3 %all-gather = f16[256,1408]{1,0:T(8,128)(2,1)S(1)} all-gather(f16[128,1408]{1,0:T(8,128)(2,1)S(1)} %convert_element_type.12), channel_id=2, replica_groups={{0,32},{33,65},{64,96},{97,129},{128,160},{161,193},{192,224},{225,257}..., dimensions={0}, use_global_device_ids=true | all-gather | bytes 1081344 | tf_op jit(solution)/shard_map/all_gather | solution.py:104
  36.3 0.1 convert.got
  36.4 0.3 fold.1
  36.7 23.9 %all_to_all.16 = f16[16,8,1408]{2,1,0:T(8,128)(2,1)S(1)} all-to-all(f16[16,8,1408]{2,1,0:T(8,128)(2,1)S(1)} %convert_bitcast_fusion), channel_id=1, replica_groups=mesh['far'=8,'pair'=2,'chip'=16,'core'=2] {'far','pair'}, dimensions={0} | all-to-all | bytes 720896 | tf_op jit(solution)/shard_map/all_to_all | solution.py:36
  60.6 0.2 activations.1
  60.8 31.1 %all_gather.23.pieces = bf16[16,8,2816]{2,1,0:T(8,128)(2,1)S(1)} all-gather(bf16[1,8,2816]{2,1,0:T(8,128)(2,1)S(1)} %activations.1), channel_id=1, replica_groups=mesh['far'=8,'pair'=2,'chip'=16,'core'=2] {'far','pair'}, dimensions={0}, use_global_device_ids=true | all-gather | bytes 765952 | tf_op jit(solution)/shard_map/all_gather | solution.py:258
  91.9 1.2 %block_inputs.1 = bf16[128,512]{1,0:T(8,128)(2,1)} custom-call(bf16[16,8,2816]{2,1,0:T(8,128)(2,1)S(1)} %all_gather.23.pieces, bf16[1344,512]{1,0:T(8,128)(2,1)S(1)} %pad_maximum_fusion.refs_0_.own, bf16[1344,512]{1,0:T(8,128)(2,1)S(1)} %collective-permute-done.refs_1_.theirs), custom_call_target="tpu_custom_call" | custom-call | tf_op jit(solution)/shard_map/block_inputs/pallas_call | solution.py:168
  93.1 3.5 %all-to-all-start.2 = ((bf16[16,8,512]{2,1,0:T(8,128)(2,1)}), bf16[16,8,512]{2,1,0:T(8,128)(2,1)S(1)}, u32[]{:S(2)}, u32[]{:S(2)}) async-start(bf16[16,8,512]{2,1,0:T(8,128)(2,1)} %bitcast.5), calls=%async_computation.2 | async-start | bytes 262144 | tf_op jit(solution)/shard_map/all_to_all | solution.py:36
  96.7 12.3 %all-gather.2 = bf16[256,1408]{1,0:T(8,128)(2,1)S(1)} all-gather(bf16[128,1408]{1,0:T(8,128)(2,1)S(1)} %given.1), channel_id=4, replica_groups=mesh['far'=8,'pair'=2,'chip'=16,'core'=2] {'core'}, dimensions={0}, use_global_device_ids=true | all-gather | bytes 1081344 | tf_op jit(solution)/shard_map/all_gather | solution.py:262
  109.0 2.2 %all-gather.1 = bf16[256,1024]{1,0:T(8,128)(2,1)S(1)} all-gather(bf16[128,1024]{1,0:T(8,128)(2,1)S(1)} %bitcast.13), channel_id=3, replica_groups=mesh['far'=8,'pair'=2,'chip'=16,'core'=2] {'core'}, dimensions={0}, use_global_device_ids=true | all-gather | bytes 786432 | tf_op jit(solution)/shard_map/all_gather | solution.py:263
  111.1 1.7 %weight_grads.1 = (bf16[448,512]{1,0:T(8,128)(2,1)}, bf16[448,512]{1,0:T(8,128)(2,1)}, bf16[448,512]{1,0:T(8,128)(2,1)}) custom-call(bf16[2,128,1024]{2,1,0:T(8,128)(2,1)S(1)} %bitcast.15, bf16[16,8,2816]{2,1,0:T(8,128)(2,1)S(1)} %all_gather.23.pieces, bf16[2,128,1408]{2,1,0:T(8,128)(2,1)S(1)} %bitcast.14), custom_call_target="tpu_custom_call" | custom-call | flops 704643072 | bytes 4194304 | tf_op jit(solution)/shard_map/weight_grads/pallas_call | solution.py:216
  112.9 0.0 all-to-all-done.2.blocks
  112.9 0.6 final_sum.1
  (6 shorter events, 0.2 us)
Async XLA Ops:
  0.6 10.2 %copy-start = (bf16[8,512]{1,0:T(8,128)(2,1)S(1)}, bf16[8,512]{1,0:T(8,128)(2,1)}, u32[]{:S(2)}) copy-start(bf16[8,512]{1,0:T(8,128)(2,1)} %param.6) | copy-start | bytes 24580
  0.6 10.2 %copy-start.1 = (bf16[8,512]{1,0:T(8,128)(2,1)S(1)}, bf16[8,512]{1,0:T(8,128)(2,1)}, u32[]{:S(2)}) copy-start(bf16[8,512]{1,0:T(8,128)(2,1)} %param.5) | copy-start | bytes 24580
  2.1 20.0 %collective-permute-start = (bf16[1344,512]{1,0:T(8,128)(2,1)S(1)}, bf16[1344,512]{1,0:T(8,128)(2,1)S(1)}, u32[]{:S(2)}, u32[]{:S(2)}) collective-permute-start(bf16[1344,512]{1,0:T(8,128)(2,1)S(1)} %pad_maximum_fusion.refs_0_.own), channel_id=1, source_target_pairs={{0,1},{1,0},{2,3},{3,2},{4,5},{5,4},{6,7},{7,6},{8,9},{9,8},{10,11... | collective-permute-start | bytes 4128776 | tf_op jit(solution)/shard_map/ppermute | solution.py:254
  93.1 19.8 %all-to-all-start.2 = ((bf16[16,8,512]{2,1,0:T(8,128)(2,1)}), bf16[16,8,512]{2,1,0:T(8,128)(2,1)S(1)}, u32[]{:S(2)}, u32[]{:S(2)}) async-start(bf16[16,8,512]{2,1,0:T(8,128)(2,1)} %bitcast.5), calls=%async_computation.2 | async-start | bytes 262144 | tf_op jit(solution)/shard_map/all_to_all | solution.py:36

commit v8 on v7

--- a/solution.py
+++ b/solution.py
@@ -36,9 +36,17 @@
     return lax.all_to_all(array.reshape(pieces, -1, array.shape[-1]), axis, 0, 0)
 
 
-def partial_kernel(both, *refs):
-    own, theirs, sent, kept = refs
+def own_kernel(both, own, out):
     width, depth = own.shape[0] // 3, own.shape[1]
+    for i, side in enumerate((0, 0, 1)):
+        x = both[:, side * depth : (side + 1) * depth]
+        at = slice(i * width, (i + 1) * width)
+        out[:, at] = contract(x, own[at], 1, 1)
+
+
+def other_kernel(both, theirs, firsts, sent, kept):
+    depth = theirs.shape[1]
+    width = theirs.shape[0] // 3
     same = lax.axis_index("pair") == lax.axis_index("core")
     notes = []
     for i, side in enumerate((0, 0, 1)):
@@ -50,7 +58,7 @@
             scale = jnp.exp2(SHIFT - exp)
             notes.append(jnp.broadcast_to(exp, (sent.shape[0], NOTE // 2)))
         at = slice(i * width, (i + 1) * width)
-        first = contract(x, own[at], 1, 1)
+        first = firsts[:, at]
         second = contract(x, theirs[at], 1, 1)
         kept[:, at] = jnp.where(same, first, second)
         sent[:, at] = jnp.where(same, second, first) * scale
@@ -61,14 +69,25 @@
 
 def partial_sums(both, own, theirs):
     tokens, width = both.shape[0], own.shape[0] // 3
-    return pl.pallas_call(
-        partial_kernel,
+    vmem = pl.BlockSpec(memory_space=pltpu.VMEM)
+    params = pltpu.CompilerParams(vmem_limit_bytes=16 << 20)
+    firsts = pl.pallas_call(
+        own_kernel,
+        out_shape=jax.ShapeDtypeStruct((tokens, 3 * width), jnp.float32),
+        in_specs=[vmem] * 2,
+        out_specs=vmem,
+        compiler_params=params,
+        cost_estimate=pl.CostEstimate(flops=10**11, bytes_accessed=3 << 20, transcendentals=0),
+        name="own_sums",
+    )(both, own)
+    return pl.pallas_call(
+        other_kernel,
         out_shape=[jax.ShapeDtypeStruct((tokens, 3 * width + NOTE), jnp.float32)] * 2,
-        in_specs=[pl.BlockSpec(memory_space=pltpu.VMEM)] * 3,
-        out_specs=[pl.BlockSpec(memory_space=pltpu.VMEM)] * 2,
-        compiler_params=pltpu.CompilerParams(vmem_limit_bytes=16 << 20),
-        name="partial_sums",
-    )(both, own, theirs)
+        in_specs=[vmem] * 3,
+        out_specs=[vmem] * 2,
+        compiler_params=params,
+        name="other_sums",
+    )(both, theirs, firsts)
 
 
 def exponents(block):
@@ -202,8 +221,9 @@
     for which, side in ((2, 1), (0, 0), (1, 0)):
         units = slice(which * width, (which + 1) * width)
         features = slice(side * depth, (side + 1) * depth)
-        total = contract(piece(mine, which, width), both[core, :, features], 0, 0)
-        total += contract(got[1 - core, :, units], both[1 - core, :, features], 0, 0)
+        delta = jnp.concatenate([piece(mine, which, width), got[1 - core, :, units]], axis=0)
+        x = jnp.concatenate([both[core, :, features], both[1 - core, :, features]], axis=0)
+        total = contract(delta, x, 0, 0)
         hold[which] = total.astype(hold.dtype)
         stores.append(pltpu.make_async_copy(hold.at[which], outs[which], sems.at[which]))
         stores[-1].start()
@@ -247,7 +267,9 @@
 
 def on_device(rows, chips, inputs, out_grad, w_gate, w_up, w_down):
     width = w_gate.shape[1]
-    own = jnp.concatenate([w_gate.T, w_up.T, w_down], axis=0)
+    own = jnp.zeros((3 * width, w_down.shape[1]), w_down.dtype)
+    for i, w in enumerate((w_gate.T, w_up.T, w_down)):
+        own = lax.dynamic_update_slice(own, w, (i * width, 0))
     copies = jnp.concatenate([inputs, out_grad], axis=1)
     copies = jnp.broadcast_to(copies[None], (chips, *copies.shape))
     both = lax.all_to_all(copies, "chip", 0, 0).reshape(-1, copies.shape[2])

time: 114 us -> 113 us (level)
  blocking collectives: 93.8 us -> 82.7 us
  starting transfers between devices: 12.3 us -> 19.6 us
  local copies, waits for them, and re-layouts: 0.03 us -> 2.6 us
  waiting for transfers between devices: 0.01 us -> 2.18 us
    all_to_all x1 -> x0, blocking collectives: 11.1 us -> none  [on_device(): both = lax.all_to_all(copies, 'chip', 0, 0).reshape(-1, copies.shape[2])]
    all_to_all x0 -> x1, starting transfers between devices: none -> 7.58 us  [on_device(): both = lax.all_to_all(copies, 'chip', 0, 0).reshape(-1, copies.shape[2])]
    ppermute x1, starting transfers between devices: 8.79 us -> 4.74 us  [on_device(): theirs = lax.ppermute(own, 'core', SWAP)]
    all_to_all x1, starting transfers between devices: 3.51 us -> 7.24 us  [exchange(): lax.all_to_all(array.reshape(pieces, -1, array.shape[-1]), axis, 0, 0)]
    all_to_all x0 -> x1, waiting for transfers between devices: none -> 1.65 us  [on_device(): both = lax.all_to_all(copies, 'chip', 0, 0).reshape(-1, copies.shape[2])]
    all_gather x1, blocking collectives: 31.1 us -> 29.7 us  [on_device(): pieces = lax.all_gather(payload, ROW, axis=0, tiled=True)]
    concatenate x1 -> x0, other arithmetic: 1.4 us -> none  [on_device(): own = jnp.concatenate([w_gate.T, w_up.T, w_down], axis=0)]
    dynamic_update_slice x0 -> x3, local copies, waits for them, and re-layouts: none -> 1.23 us  [on_device(): own = lax.dynamic_update_slice(own, w, (i * width, 0))]
  transfers between devices with their start and end apart: 2 -> 3, of which waited for: 0 -> 2; matrix products, arithmetic and copies ran while one was open for 0% -> 1% of each run, Pallas kernels for 2% -> 2%
where the time goes in v8:
time: 113 us
  blocking collectives  82.7 us (73%)
  starting transfers between devices  19.6 us (17%)
  Pallas kernels  4.19 us (4%)
  local copies, waits for them, and re-layouts  2.6 us (2%)
  waiting for transfers between devices  2.18 us (2%)
    all_gather x1, blocking collectives, on_device(): pieces = lax.all_gather(payload, ROW, axis=0, tiled=True)  29.7 us
    all_to_all x1, blocking collectives, exchange(): lax.all_to_all(array.reshape(pieces, -1, array.shape[-1]), axis, 0, 0)  24.1 us
    all_gather x1, blocking collectives, fold(): lax.all_gather(sent.astype(jnp.float16), (*ROW, 'core'), axis=0, axis_ind...  14.2 us
    all_gather x1, blocking collectives, on_device(): got = lax.all_gather(given(pieces), 'core', axis=0)  12.5 us
    all_to_all x1, starting transfers between devices, on_device(): both = lax.all_to_all(copies, 'chip', 0, 0).reshape(-1, copies.shape[2])  7.58 us
    all_to_all x1, starting transfers between devices, exchange(): lax.all_to_all(array.reshape(pieces, -1, array.shape[-1]), axis, 0, 0)  7.24 us
    ppermute x1, starting transfers between devices, on_device(): theirs = lax.ppermute(own, 'core', SWAP)  4.74 us
  transfers between devices with their start and end apart: 3, of which 2 were waited for; matrix products, arithmetic and copies ran while one was open for 1% of the time, Pallas kernels for 2%

profile of v8, /device:TPU:1, one launch (start us, length us, event | category | flops | bytes accessed | tf_op | source)
XLA Modules:
  0.0 113.0 jit_solution(13456022657422058304)
XLA Ops:
  0.6 0.8 pad_maximum_fusion
  1.4 0.7 broadcast_in_dim.2
  2.1 7.6 %all-to-all-start = ((bf16[16,8,1024]{2,1,0:T(8,128)(2,1)}), bf16[16,8,1024]{2,1,0:T(8,128)(2,1)S(1)}, u32[]{:S(2)}, u32[]{:S(2)}) async-start(bf16[16,8,1024]{2,1,0:T(8,128)(2,1)} %broadcast_in_dim.2), calls=%async_computation | async-start | bytes 524288 | tf_op jit(solution)/shard_map/all_to_all | solution.py:275
  9.7 0.0 copy-start.4
  9.7 1.2 %dynamic_update_slice.9 = bf16[1344,512]{1,0:T(8,128)(2,1)S(1)} pad(bf16[448,512]{1,0:T(8,128)(2,1)} %bitcast.20, bf16[]{:T(256)} %constant.0.clone.1), padding=0_896x0_0 | pad | bytes 1835010 | tf_op jit(solution)/shard_map/dynamic_update_slice | solution.py:272
  11.0 4.7 %collective-permute-start = (bf16[1344,512]{1,0:T(8,128)(2,1)S(1)}, bf16[1344,512]{1,0:T(8,128)(2,1)S(1)}, u32[]{:S(2)}, u32[]{:S(2)}) collective-permute-start(bf16[1344,512]{1,0:T(8,128)(2,1)S(1)} %constant_dynamic-update-slice_fusion.own), channel_id=1, source_target_pairs={{0,1},{1,0},{2,3},{3,2},{4,5},{5,4},{6,7},{7,6},{8,9},{9,8},{10,11... | collective-permute-start | bytes 4128776 | tf_op jit(solution)/shard_map/ppermute | solution.py:276
  15.8 1.6 %all-to-all-done = bf16[16,8,1024]{2,1,0:T(8,128)(2,1)S(1)} async-done(((bf16[16,8,1024]{2,1,0:T(8,128)(2,1)}), bf16[16,8,1024]{2,1,0:T(8,128)(2,1)S(1)}, u32[]{:S(2)}, u32[]{:S(2)}) %all-to-all-start) | async-done | bytes 262176 | tf_op jit(solution)/shard_map/all_to_all | solution.py:275
  17.4 0.5 own_sums.1.firsts
  18.0 0.5 collective-permute-done.theirs
  18.5 0.6 other_sums.1
  19.2 14.2 %all-gather = f16[256,1408]{1,0:T(8,128)(2,1)S(1)} all-gather(f16[128,1408]{1,0:T(8,128)(2,1)S(1)} %convert_element_type.12), channel_id=2, replica_groups={{0,32},{33,65},{64,96},{97,129},{128,160},{161,193},{192,224},{225,257}..., dimensions={0}, use_global_device_ids=true | all-gather | bytes 1081344 | tf_op jit(solution)/shard_map/all_gather | solution.py:123
  33.3 0.1 convert.got
  33.4 0.3 fold.1
  33.8 24.1 %all_to_all.15 = f16[16,8,1408]{2,1,0:T(8,128)(2,1)S(1)} all-to-all(f16[16,8,1408]{2,1,0:T(8,128)(2,1)S(1)} %convert_bitcast_fusion), channel_id=1, replica_groups=mesh['far'=8,'pair'=2,'chip'=16,'core'=2] {'far','pair'}, dimensions={0} | all-to-all | bytes 720896 | tf_op jit(solution)/shard_map/all_to_all | solution.py:36
  57.9 0.2 activations.1
  58.1 29.7 %all_gather.23.pieces = bf16[16,8,2816]{2,1,0:T(8,128)(2,1)S(1)} all-gather(bf16[1,8,2816]{2,1,0:T(8,128)(2,1)S(1)} %activations.1), channel_id=1, replica_groups=mesh['far'=8,'pair'=2,'chip'=16,'core'=2] {'far','pair'}, dimensions={0}, use_global_device_ids=true | all-gather | bytes 765952 | tf_op jit(solution)/shard_map/all_gather | solution.py:280
  87.8 0.5 block_inputs.1
  88.3 0.6 copy-done.2
  88.9 7.2 %all-to-all-start.2 = ((bf16[16,8,512]{2,1,0:T(8,128)(2,1)}), bf16[16,8,512]{2,1,0:T(8,128)(2,1)S(1)}, u32[]{:S(2)}, u32[]{:S(2)}) async-start(bf16[16,8,512]{2,1,0:T(8,128)(2,1)} %bitcast.17), calls=%async_computation.2 | async-start | bytes 262144 | tf_op jit(solution)/shard_map/all_to_all | solution.py:36
  96.2 12.5 %all-gather.2 = bf16[256,1408]{1,0:T(8,128)(2,1)S(1)} all-gather(bf16[128,1408]{1,0:T(8,128)(2,1)S(1)} %given.1), channel_id=4, replica_groups=mesh['far'=8,'pair'=2,'chip'=16,'core'=2] {'core'}, dimensions={0}, use_global_device_ids=true | all-gather | bytes 1081344 | tf_op jit(solution)/shard_map/all_gather | solution.py:284
  108.7 2.2 %all-gather.1 = bf16[256,1024]{1,0:T(8,128)(2,1)S(1)} all-gather(bf16[128,1024]{1,0:T(8,128)(2,1)S(1)} %bitcast.15), channel_id=3, replica_groups=mesh['far'=8,'pair'=2,'chip'=16,'core'=2] {'core'}, dimensions={0}, use_global_device_ids=true | all-gather | bytes 786432 | tf_op jit(solution)/shard_map/all_gather | solution.py:285
  110.9 1.4 %weight_grads.1 = (bf16[448,512]{1,0:T(8,128)(2,1)}, bf16[448,512]{1,0:T(8,128)(2,1)}, bf16[448,512]{1,0:T(8,128)(2,1)}) custom-call(bf16[2,128,1024]{2,1,0:T(8,128)(2,1)S(1)} %bitcast.18, bf16[16,8,2816]{2,1,0:T(8,128)(2,1)S(1)} %all_gather.23.pieces, bf16[2,128,1408]{2,1,0:T(8,128)(2,1)S(1)} %bitcast.16), custom_call_target="tpu_custom_call" | custom-call | flops 704643072 | bytes 4194304 | tf_op jit(solution)/shard_map/weight_grads/pallas_call | solution.py:236
  112.3 0.0 all-to-all-done.2.blocks
  112.4 0.6 final_sum.1
  (14 shorter events, 0.2 us)
Async XLA Ops:
  0.6 10.3 %copy-start.3 = (bf16[512,448]{0,1:T(8,128)(2,1)S(1)}, bf16[512,448]{0,1:T(8,128)(2,1)}, u32[]{:S(2)}) copy-start(bf16[512,448]{0,1:T(8,128)(2,1)} %param.8) | copy-start | bytes 1376260
  2.1 15.3 %all-to-all-start = ((bf16[16,8,1024]{2,1,0:T(8,128)(2,1)}), bf16[16,8,1024]{2,1,0:T(8,128)(2,1)S(1)}, u32[]{:S(2)}, u32[]{:S(2)}) async-start(bf16[16,8,1024]{2,1,0:T(8,128)(2,1)} %broadcast_in_dim.2), calls=%async_computation | async-start | bytes 524288 | tf_op jit(solution)/shard_map/all_to_all | solution.py:275
  9.7 1.2 %copy-start.4 = (bf16[448,512]{1,0:T(8,128)(2,1)S(1)}, bf16[448,512]{1,0:T(8,128)(2,1)}, u32[]{:S(2)}) copy-start(bf16[448,512]{1,0:T(8,128)(2,1)} %param.9) | copy-start | bytes 1376260
  11.0 7.5 %collective-permute-start = (bf16[1344,512]{1,0:T(8,128)(2,1)S(1)}, bf16[1344,512]{1,0:T(8,128)(2,1)S(1)}, u32[]{:S(2)}, u32[]{:S(2)}) collective-permute-start(bf16[1344,512]{1,0:T(8,128)(2,1)S(1)} %constant_dynamic-update-slice_fusion.own), channel_id=1, source_target_pairs={{0,1},{1,0},{2,3},{3,2},{4,5},{5,4},{6,7},{7,6},{8,9},{9,8},{10,11... | collective-permute-start | bytes 4128776 | tf_op jit(solution)/shard_map/ppermute | solution.py:276
  17.4 1.1 copy-start
  88.3 0.6 copy-start.2
  88.9 19.8 %copy-start.1 = (bf16[16,8,1024]{2,1,0:T(8,128)(2,1)S(1)}, bf16[16,8,1024]{2,1,0:T(8,128)(2,1)}, u32[]{:S(2)}) copy-start(bf16[16,8,1024]{2,1,0:T(8,128)(2,1)} %copy-done) | copy-start | bytes 786436
  88.9 23.4 %all-to-all-start.2 = ((bf16[16,8,512]{2,1,0:T(8,128)(2,1)}), bf16[16,8,512]{2,1,0:T(8,128)(2,1)S(1)}, u32[]{:S(2)}, u32[]{:S(2)}) async-start(bf16[16,8,512]{2,1,0:T(8,128)(2,1)} %bitcast.17), calls=%async_computation.2 | async-start | bytes 262144 | tf_op jit(solution)/shard_map/all_to_all | solution.py:36

commit v9 on v8

--- a/solution.py
+++ b/solution.py
@@ -38,16 +38,6 @@
 
 def own_kernel(both, own, out):
     width, depth = own.shape[0] // 3, own.shape[1]
-    for i, side in enumerate((0, 0, 1)):
-        x = both[:, side * depth : (side + 1) * depth]
-        at = slice(i * width, (i + 1) * width)
-        out[:, at] = contract(x, own[at], 1, 1)
-
-
-def other_kernel(both, theirs, firsts, sent, kept):
-    depth = theirs.shape[1]
-    width = theirs.shape[0] // 3
-    same = lax.axis_index("pair") == lax.axis_index("core")
     notes = []
     for i, side in enumerate((0, 0, 1)):
         x = both[:, side * depth : (side + 1) * depth]
@@ -55,14 +45,25 @@
             largest = jnp.max(jnp.abs(x).astype(jnp.float32), axis=0, keepdims=True)
             largest = jnp.max(largest, axis=1, keepdims=True)
             exp = jnp.ceil(jnp.log2(jnp.maximum(largest, 2.0**LEAST)))
-            scale = jnp.exp2(SHIFT - exp)
-            notes.append(jnp.broadcast_to(exp, (sent.shape[0], NOTE // 2)))
+            notes.append(jnp.broadcast_to(exp, (out.shape[0], NOTE // 2)))
+        at = slice(i * width, (i + 1) * width)
+        out[:, at] = contract(x, own[at], 1, 1)
+    out[:, 3 * width :] = jnp.concatenate(notes, axis=1)
+
+
+def other_kernel(both, theirs, firsts, sent, kept):
+    depth = theirs.shape[1]
+    width = theirs.shape[0] // 3
+    same = lax.axis_index("pair") == lax.axis_index("core")
+    scales = [jnp.exp2(SHIFT - exp) for exp in exponents(firsts[...])]
+    for i, side in enumerate((0, 0, 1)):
+        x = both[:, side * depth : (side + 1) * depth]
         at = slice(i * width, (i + 1) * width)
         first = firsts[:, at]
         second = contract(x, theirs[at], 1, 1)
         kept[:, at] = jnp.where(same, first, second)
-        sent[:, at] = jnp.where(same, second, first) * scale
-    notes = jnp.concatenate(notes, axis=1)
+        sent[:, at] = jnp.where(same, second, first) * scales[side]
+    notes = firsts[:, 3 * width :]
     kept[:, 3 * width :] = notes
     sent[:, 3 * width :] = notes
 
@@ -73,7 +74,7 @@
     params = pltpu.CompilerParams(vmem_limit_bytes=16 << 20)
     firsts = pl.pallas_call(
         own_kernel,
-        out_shape=jax.ShapeDtypeStruct((tokens, 3 * width), jnp.float32),
+        out_shape=jax.ShapeDtypeStruct((tokens, 3 * width + NOTE), jnp.float32),
         in_specs=[vmem] * 2,
         out_specs=vmem,
         compiler_params=params,

time: 113 us -> 113 us (level)
  no operation moved by 1% of the time
where the time goes in v9:
time: 113 us
  blocking collectives  82.6 us (73%)
  starting transfers between devices  19.6 us (17%)
  Pallas kernels  4.18 us (4%)
  local copies, waits for them, and re-layouts  2.6 us (2%)
  waiting for transfers between devices  2.18 us (2%)
    all_gather x1, blocking collectives, on_device(): pieces = lax.all_gather(payload, ROW, axis=0, tiled=True)  29.7 us
    all_to_all x1, blocking collectives, exchange(): lax.all_to_all(array.reshape(pieces, -1, array.shape[-1]), axis, 0, 0)  24.1 us
    all_gather x1, blocking collectives, fold(): lax.all_gather(sent.astype(jnp.float16), (*ROW, 'core'), axis=0, axis_ind...  14.2 us
    all_gather x1, blocking collectives, on_device(): got = lax.all_gather(given(pieces), 'core', axis=0)  12.5 us
    all_to_all x1, starting transfers between devices, on_device(): both = lax.all_to_all(copies, 'chip', 0, 0).reshape(-1, copies.shape[2])  7.58 us
    all_to_all x1, starting transfers between devices, exchange(): lax.all_to_all(array.reshape(pieces, -1, array.shape[-1]), axis, 0, 0)  7.25 us
    ppermute x1, starting transfers between devices, on_device(): theirs = lax.ppermute(own, 'core', SWAP)  4.74 us
  transfers between devices with their start and end apart: 3, of which 2 were waited for; matrix products, arithmetic and copies ran while one was open for 1% of the time, Pallas kernels for 2%

profile of v9, /device:TPU:1, one launch (start us, length us, event | category | flops | bytes accessed | tf_op | source)
XLA Modules:
  0.0 113.0 jit_solution(17818824141564147820)
XLA Ops:
  0.6 0.8 pad_maximum_fusion
  1.4 0.7 broadcast_in_dim.2
  2.1 7.6 %all-to-all-start = ((bf16[16,8,1024]{2,1,0:T(8,128)(2,1)}), bf16[16,8,1024]{2,1,0:T(8,128)(2,1)S(1)}, u32[]{:S(2)}, u32[]{:S(2)}) async-start(bf16[16,8,1024]{2,1,0:T(8,128)(2,1)} %broadcast_in_dim.2), calls=%async_computation | async-start | bytes 524288 | tf_op jit(solution)/shard_map/all_to_all | solution.py:276
  9.7 0.0 copy-start.4
  9.7 1.2 %dynamic_update_slice.9 = bf16[1344,512]{1,0:T(8,128)(2,1)S(1)} pad(bf16[448,512]{1,0:T(8,128)(2,1)} %bitcast.20, bf16[]{:T(256)} %constant.0.clone.1), padding=0_896x0_0 | pad | bytes 1835010 | tf_op jit(solution)/shard_map/dynamic_update_slice | solution.py:273
  11.0 4.7 %collective-permute-start = (bf16[1344,512]{1,0:T(8,128)(2,1)S(1)}, bf16[1344,512]{1,0:T(8,128)(2,1)S(1)}, u32[]{:S(2)}, u32[]{:S(2)}) collective-permute-start(bf16[1344,512]{1,0:T(8,128)(2,1)S(1)} %constant_dynamic-update-slice_fusion.own), channel_id=1, source_target_pairs={{0,1},{1,0},{2,3},{3,2},{4,5},{5,4},{6,7},{7,6},{8,9},{9,8},{10,11... | collective-permute-start | bytes 4128776 | tf_op jit(solution)/shard_map/ppermute | solution.py:277
  15.8 1.6 %all-to-all-done = bf16[16,8,1024]{2,1,0:T(8,128)(2,1)S(1)} async-done(((bf16[16,8,1024]{2,1,0:T(8,128)(2,1)}), bf16[16,8,1024]{2,1,0:T(8,128)(2,1)S(1)}, u32[]{:S(2)}, u32[]{:S(2)}) %all-to-all-start) | async-done | bytes 262176 | tf_op jit(solution)/shard_map/all_to_all | solution.py:276
  17.4 0.5 own_sums.1.firsts
  18.0 0.5 collective-permute-done.theirs
  18.5 0.6 other_sums.1
  19.1 14.2 %all-gather = f16[256,1408]{1,0:T(8,128)(2,1)S(1)} all-gather(f16[128,1408]{1,0:T(8,128)(2,1)S(1)} %convert_element_type.12), channel_id=2, replica_groups={{0,32},{33,65},{64,96},{97,129},{128,160},{161,193},{192,224},{225,257}..., dimensions={0}, use_global_device_ids=true | all-gather | bytes 1081344 | tf_op jit(solution)/shard_map/all_gather | solution.py:124
  33.3 0.1 convert.got
  33.4 0.3 fold.1
  33.7 24.1 %all_to_all.15 = f16[16,8,1408]{2,1,0:T(8,128)(2,1)S(1)} all-to-all(f16[16,8,1408]{2,1,0:T(8,128)(2,1)S(1)} %convert_bitcast_fusion), channel_id=1, replica_groups=mesh['far'=8,'pair'=2,'chip'=16,'core'=2] {'far','pair'}, dimensions={0} | all-to-all | bytes 720896 | tf_op jit(solution)/shard_map/all_to_all | solution.py:36
  57.9 0.2 activations.1
  58.1 29.7 %all_gather.23.pieces = bf16[16,8,2816]{2,1,0:T(8,128)(2,1)S(1)} all-gather(bf16[1,8,2816]{2,1,0:T(8,128)(2,1)S(1)} %activations.1), channel_id=1, replica_groups=mesh['far'=8,'pair'=2,'chip'=16,'core'=2] {'far','pair'}, dimensions={0}, use_global_device_ids=true | all-gather | bytes 765952 | tf_op jit(solution)/shard_map/all_gather | solution.py:281
  87.8 0.5 block_inputs.1
  88.3 0.6 copy-done.2
  88.9 7.2 %all-to-all-start.2 = ((bf16[16,8,512]{2,1,0:T(8,128)(2,1)}), bf16[16,8,512]{2,1,0:T(8,128)(2,1)S(1)}, u32[]{:S(2)}, u32[]{:S(2)}) async-start(bf16[16,8,512]{2,1,0:T(8,128)(2,1)} %bitcast.17), calls=%async_computation.2 | async-start | bytes 262144 | tf_op jit(solution)/shard_map/all_to_all | solution.py:36
  96.2 12.5 %all-gather.2 = bf16[256,1408]{1,0:T(8,128)(2,1)S(1)} all-gather(bf16[128,1408]{1,0:T(8,128)(2,1)S(1)} %given.1), channel_id=4, replica_groups=mesh['far'=8,'pair'=2,'chip'=16,'core'=2] {'core'}, dimensions={0}, use_global_device_ids=true | all-gather | bytes 1081344 | tf_op jit(solution)/shard_map/all_gather | solution.py:285
  108.7 2.2 %all-gather.1 = bf16[256,1024]{1,0:T(8,128)(2,1)S(1)} all-gather(bf16[128,1024]{1,0:T(8,128)(2,1)S(1)} %bitcast.15), channel_id=3, replica_groups=mesh['far'=8,'pair'=2,'chip'=16,'core'=2] {'core'}, dimensions={0}, use_global_device_ids=true | all-gather | bytes 786432 | tf_op jit(solution)/shard_map/all_gather | solution.py:286
  110.9 1.4 %weight_grads.1 = (bf16[448,512]{1,0:T(8,128)(2,1)}, bf16[448,512]{1,0:T(8,128)(2,1)}, bf16[448,512]{1,0:T(8,128)(2,1)}) custom-call(bf16[2,128,1024]{2,1,0:T(8,128)(2,1)S(1)} %bitcast.18, bf16[16,8,2816]{2,1,0:T(8,128)(2,1)S(1)} %all_gather.23.pieces, bf16[2,128,1408]{2,1,0:T(8,128)(2,1)S(1)} %bitcast.16), custom_call_target="tpu_custom_call" | custom-call | flops 704643072 | bytes 4194304 | tf_op jit(solution)/shard_map/weight_grads/pallas_call | solution.py:237
  112.3 0.0 all-to-all-done.2.blocks
  112.3 0.6 final_sum.1
  (14 shorter events, 0.2 us)
Async XLA Ops:
  0.6 10.3 %copy-start.3 = (bf16[512,448]{0,1:T(8,128)(2,1)S(1)}, bf16[512,448]{0,1:T(8,128)(2,1)}, u32[]{:S(2)}) copy-start(bf16[512,448]{0,1:T(8,128)(2,1)} %param.8) | copy-start | bytes 1376260
  2.1 15.3 %all-to-all-start = ((bf16[16,8,1024]{2,1,0:T(8,128)(2,1)}), bf16[16,8,1024]{2,1,0:T(8,128)(2,1)S(1)}, u32[]{:S(2)}, u32[]{:S(2)}) async-start(bf16[16,8,1024]{2,1,0:T(8,128)(2,1)} %broadcast_in_dim.2), calls=%async_computation | async-start | bytes 524288 | tf_op jit(solution)/shard_map/all_to_all | solution.py:276
  9.7 1.2 %copy-start.4 = (bf16[448,512]{1,0:T(8,128)(2,1)S(1)}, bf16[448,512]{1,0:T(8,128)(2,1)}, u32[]{:S(2)}) copy-start(bf16[448,512]{1,0:T(8,128)(2,1)} %param.9) | copy-start | bytes 1376260
  11.0 7.5 %collective-permute-start = (bf16[1344,512]{1,0:T(8,128)(2,1)S(1)}, bf16[1344,512]{1,0:T(8,128)(2,1)S(1)}, u32[]{:S(2)}, u32[]{:S(2)}) collective-permute-start(bf16[1344,512]{1,0:T(8,128)(2,1)S(1)} %constant_dynamic-update-slice_fusion.own), channel_id=1, source_target_pairs={{0,1},{1,0},{2,3},{3,2},{4,5},{5,4},{6,7},{7,6},{8,9},{9,8},{10,11... | collective-permute-start | bytes 4128776 | tf_op jit(solution)/shard_map/ppermute | solution.py:277
  17.4 1.1 copy-start
  88.3 0.6 copy-start.2
  88.9 19.8 %copy-start.1 = (bf16[16,8,1024]{2,1,0:T(8,128)(2,1)S(1)}, bf16[16,8,1024]{2,1,0:T(8,128)(2,1)}, u32[]{:S(2)}) copy-start(bf16[16,8,1024]{2,1,0:T(8,128)(2,1)} %copy-done) | copy-start | bytes 786436
  88.9 23.4 %all-to-all-start.2 = ((bf16[16,8,512]{2,1,0:T(8,128)(2,1)}), bf16[16,8,512]{2,1,0:T(8,128)(2,1)S(1)}, u32[]{:S(2)}, u32[]{:S(2)}) async-start(bf16[16,8,512]{2,1,0:T(8,128)(2,1)} %bitcast.17), calls=%async_computation.2 | async-start | bytes 262144 | tf_op jit(solution)/shard_map/all_to_all | solution.py:36

commit v10 on v8

--- a/solution.py
+++ b/solution.py
@@ -172,9 +172,10 @@
     return pieces[:, :, pl.ds(pl.multiple_of(core * stride, 128), stride)]
 
 
-def block_kernel(pieces, own, theirs, out):
+def block_kernel(pieces, own, theirs, out, given):
     width = own.shape[0] // 3
     core = lax.axis_index("core")
+    given[...] = of_core(pieces, 1 - core).reshape(given.shape)
     total = 0.0
     for c, weights in ((core, own), (1 - core, theirs)):
         part = of_core(pieces, c)
@@ -186,30 +187,15 @@
 def block_inputs(pieces, own, theirs):
     return pl.pallas_call(
         block_kernel,
-        out_shape=jax.ShapeDtypeStruct(
-            (pieces.shape[0] * pieces.shape[1], own.shape[1]), jnp.bfloat16
-        ),
+        out_shape=[
+            jax.ShapeDtypeStruct((pieces.shape[0] * pieces.shape[1], columns), jnp.bfloat16)
+            for columns in (own.shape[1], pieces.shape[2] // 2)
+        ],
         in_specs=[pl.BlockSpec(memory_space=pltpu.VMEM)] * 3,
-        out_specs=pl.BlockSpec(memory_space=pltpu.VMEM),
+        out_specs=[pl.BlockSpec(memory_space=pltpu.VMEM)] * 2,
         compiler_params=pltpu.CompilerParams(vmem_limit_bytes=16 << 20),
         name="block_inputs",
     )(pieces, own, theirs)
-
-
-def give_kernel(pieces, out):
-    out[...] = of_core(pieces, 1 - lax.axis_index("core")).reshape(out.shape)
-
-
-def given(pieces):
-    shape = (pieces.shape[0] * pieces.shape[1], pieces.shape[2] // 2)
-    return pl.pallas_call(
-        give_kernel,
-        out_shape=jax.ShapeDtypeStruct(shape, jnp.bfloat16),
-        in_specs=[pl.BlockSpec(memory_space=pltpu.VMEM)],
-        out_specs=pl.BlockSpec(memory_space=pltpu.VMEM),
-        compiler_params=pltpu.CompilerParams(vmem_limit_bytes=16 << 20),
-        name="given",
-    )(pieces)
 
 
 def grad_kernel(both, pieces, got, *refs):
@@ -278,10 +264,10 @@
     blocks = exchange(partial.astype(jnp.float16), ROW, rows)
     payload = activations(blocks.astype(jnp.float32))
     pieces = lax.all_gather(payload, ROW, axis=0, tiled=True)
-    block_in = block_inputs(pieces, own, theirs)
-    block_in, pieces, both = lax.optimization_barrier((block_in, pieces, both))
+    block_in, given = block_inputs(pieces, own, theirs)
+    block_in, given, both = lax.optimization_barrier((block_in, given, both))
     block_in = exchange(block_in, "chip", chips)
-    got = lax.all_gather(given(pieces), "core", axis=0)
+    got = lax.all_gather(given, "core", axis=0)
     grads = weight_grads(lax.all_gather(both, "core", axis=0), pieces, got, width)
     block_in, grad_gate, grad_up, grad_down = lax.optimization_barrier((block_in, *grads))
     grad_inputs = final_sum(block_in)

time: 113 us -> 114 us (level)
  no operation moved by 1% of the time
where the time goes in v10:
time: 114 us
  blocking collectives  82.9 us (73%)
  starting transfers between devices  19.5 us (17%)
  Pallas kernels  4.17 us (4%)
  local copies, waits for them, and re-layouts  3.35 us (3%)
  waiting for transfers between devices  2.18 us (2%)
    all_gather x1, blocking collectives, on_device(): pieces = lax.all_gather(payload, ROW, axis=0, tiled=True)  29.7 us
    all_to_all x1, blocking collectives, exchange(): lax.all_to_all(array.reshape(pieces, -1, array.shape[-1]), axis, 0, 0)  24.1 us
    all_gather x1, blocking collectives, fold(): lax.all_gather(sent.astype(jnp.float16), (*ROW, 'core'), axis=0, axis_ind...  14.2 us
    all_gather x1, blocking collectives, on_device(): got = lax.all_gather(given, 'core', axis=0)  12.7 us
    all_to_all x1, starting transfers between devices, on_device(): both = lax.all_to_all(copies, 'chip', 0, 0).reshape(-1, copies.shape[2])  7.58 us
    all_to_all x1, starting transfers between devices, exchange(): lax.all_to_all(array.reshape(pieces, -1, array.shape[-1]), axis, 0, 0)  7.22 us
    ppermute x1, starting transfers between devices, on_device(): theirs = lax.ppermute(own, 'core', SWAP)  4.74 us
  transfers between devices with their start and end apart: 3, of which 2 were waited for; matrix products, arithmetic and copies ran while one was open for 1% of the time, Pallas kernels for 2%

profile of v10, /device:TPU:1, one launch (start us, length us, event | category | flops | bytes accessed | tf_op | source)
XLA Modules:
  0.0 113.9 jit_solution(13615085784154764570)
XLA Ops:
  0.6 0.8 pad_maximum_fusion
  1.4 0.7 broadcast_in_dim.2
  2.1 7.6 %all-to-all-start = ((bf16[16,8,1024]{2,1,0:T(8,128)(2,1)}), bf16[16,8,1024]{2,1,0:T(8,128)(2,1)S(1)}, u32[]{:S(2)}, u32[]{:S(2)}) async-start(bf16[16,8,1024]{2,1,0:T(8,128)(2,1)} %broadcast_in_dim.2), calls=%async_computation | async-start | bytes 524288 | tf_op jit(solution)/shard_map/all_to_all | solution.py:261
  9.7 0.0 copy-start.5
  9.7 1.2 %dynamic_update_slice.9 = bf16[1344,512]{1,0:T(8,128)(2,1)S(1)} pad(bf16[448,512]{1,0:T(8,128)(2,1)} %bitcast.20, bf16[]{:T(256)} %constant.0.clone.1), padding=0_896x0_0 | pad | bytes 1835010 | tf_op jit(solution)/shard_map/dynamic_update_slice | solution.py:258
  11.0 4.7 %collective-permute-start = (bf16[1344,512]{1,0:T(8,128)(2,1)S(1)}, bf16[1344,512]{1,0:T(8,128)(2,1)S(1)}, u32[]{:S(2)}, u32[]{:S(2)}) collective-permute-start(bf16[1344,512]{1,0:T(8,128)(2,1)S(1)} %constant_dynamic-update-slice_fusion.own), channel_id=1, source_target_pairs={{0,1},{1,0},{2,3},{3,2},{4,5},{5,4},{6,7},{7,6},{8,9},{9,8},{10,11... | collective-permute-start | bytes 4128776 | tf_op jit(solution)/shard_map/ppermute | solution.py:262
  15.8 1.6 %all-to-all-done = bf16[16,8,1024]{2,1,0:T(8,128)(2,1)S(1)} async-done(((bf16[16,8,1024]{2,1,0:T(8,128)(2,1)}), bf16[16,8,1024]{2,1,0:T(8,128)(2,1)S(1)}, u32[]{:S(2)}, u32[]{:S(2)}) %all-to-all-start) | async-done | bytes 262176 | tf_op jit(solution)/shard_map/all_to_all | solution.py:261
  17.4 0.5 own_sums.1.firsts
  18.0 0.5 collective-permute-done.theirs
  18.5 0.6 other_sums.1
  19.2 14.2 %all-gather = f16[256,1408]{1,0:T(8,128)(2,1)S(1)} all-gather(f16[128,1408]{1,0:T(8,128)(2,1)S(1)} %convert_element_type.12), channel_id=2, replica_groups={{0,32},{33,65},{64,96},{97,129},{128,160},{161,193},{192,224},{225,257}..., dimensions={0}, use_global_device_ids=true | all-gather | bytes 1081344 | tf_op jit(solution)/shard_map/all_gather | solution.py:123
  33.3 0.1 convert.got
  33.4 0.3 fold.1
  33.8 24.1 %all_to_all.15 = f16[16,8,1408]{2,1,0:T(8,128)(2,1)S(1)} all-to-all(f16[16,8,1408]{2,1,0:T(8,128)(2,1)S(1)} %convert_bitcast_fusion), channel_id=1, replica_groups=mesh['far'=8,'pair'=2,'chip'=16,'core'=2] {'far','pair'}, dimensions={0} | all-to-all | bytes 720896 | tf_op jit(solution)/shard_map/all_to_all | solution.py:36
  57.9 0.2 activations.1
  58.1 29.7 %all_gather.23.pieces = bf16[16,8,2816]{2,1,0:T(8,128)(2,1)S(1)} all-gather(bf16[1,8,2816]{2,1,0:T(8,128)(2,1)S(1)} %activations.1), channel_id=1, replica_groups=mesh['far'=8,'pair'=2,'chip'=16,'core'=2] {'far','pair'}, dimensions={0}, use_global_device_ids=true | all-gather | bytes 765952 | tf_op jit(solution)/shard_map/all_gather | solution.py:266
  87.8 0.5 block_inputs.1
  88.3 0.7 copy-done.2
  89.1 0.6 copy-done.3
  89.7 7.2 %all-to-all-start.2 = ((bf16[16,8,512]{2,1,0:T(8,128)(2,1)}), bf16[16,8,512]{2,1,0:T(8,128)(2,1)S(1)}, u32[]{:S(2)}, u32[]{:S(2)}) async-start(bf16[16,8,512]{2,1,0:T(8,128)(2,1)} %bitcast.18), calls=%async_computation.2 | async-start | bytes 262144 | tf_op jit(solution)/shard_map/all_to_all | solution.py:36
  96.9 12.7 %all-gather.2 = bf16[256,1408]{1,0:T(8,128)(2,1)S(1)} all-gather(bf16[128,1408]{1,0:T(8,128)(2,1)} %copy-done.2), channel_id=4, replica_groups=mesh['far'=8,'pair'=2,'chip'=16,'core'=2] {'core'}, dimensions={0}, use_global_device_ids=true | all-gather | bytes 1081344 | tf_op jit(solution)/shard_map/all_gather | solution.py:270
  109.7 2.2 %all-gather.1 = bf16[256,1024]{1,0:T(8,128)(2,1)S(1)} all-gather(bf16[128,1024]{1,0:T(8,128)(2,1)S(1)} %bitcast.15), channel_id=3, replica_groups=mesh['far'=8,'pair'=2,'chip'=16,'core'=2] {'core'}, dimensions={0}, use_global_device_ids=true | all-gather | bytes 786432 | tf_op jit(solution)/shard_map/all_gather | solution.py:271
  111.8 1.4 %weight_grads.1 = (bf16[448,512]{1,0:T(8,128)(2,1)}, bf16[448,512]{1,0:T(8,128)(2,1)}, bf16[448,512]{1,0:T(8,128)(2,1)}) custom-call(bf16[2,128,1024]{2,1,0:T(8,128)(2,1)S(1)} %bitcast.17, bf16[16,8,2816]{2,1,0:T(8,128)(2,1)S(1)} %all_gather.23.pieces, bf16[2,128,1408]{2,1,0:T(8,128)(2,1)S(1)} %bitcast.16), custom_call_target="tpu_custom_call" | custom-call | flops 704643072 | bytes 4194304 | tf_op jit(solution)/shard_map/weight_grads/pallas_call | solution.py:222
  113.3 0.6 final_sum.1
  (15 shorter events, 0.2 us)
Async XLA Ops:
  0.6 10.3 %copy-start.4 = (bf16[512,448]{0,1:T(8,128)(2,1)S(1)}, bf16[512,448]{0,1:T(8,128)(2,1)}, u32[]{:S(2)}) copy-start(bf16[512,448]{0,1:T(8,128)(2,1)} %param.8) | copy-start | bytes 1376260
  2.1 15.3 %all-to-all-start = ((bf16[16,8,1024]{2,1,0:T(8,128)(2,1)}), bf16[16,8,1024]{2,1,0:T(8,128)(2,1)S(1)}, u32[]{:S(2)}, u32[]{:S(2)}) async-start(bf16[16,8,1024]{2,1,0:T(8,128)(2,1)} %broadcast_in_dim.2), calls=%async_computation | async-start | bytes 524288 | tf_op jit(solution)/shard_map/all_to_all | solution.py:261
  9.7 1.2 %copy-start.5 = (bf16[448,512]{1,0:T(8,128)(2,1)S(1)}, bf16[448,512]{1,0:T(8,128)(2,1)}, u32[]{:S(2)}) copy-start(bf16[448,512]{1,0:T(8,128)(2,1)} %param.9) | copy-start | bytes 1376260
  11.0 7.5 %collective-permute-start = (bf16[1344,512]{1,0:T(8,128)(2,1)S(1)}, bf16[1344,512]{1,0:T(8,128)(2,1)S(1)}, u32[]{:S(2)}, u32[]{:S(2)}) collective-permute-start(bf16[1344,512]{1,0:T(8,128)(2,1)S(1)} %constant_dynamic-update-slice_fusion.own), channel_id=1, source_target_pairs={{0,1},{1,0},{2,3},{3,2},{4,5},{5,4},{6,7},{7,6},{8,9},{9,8},{10,11... | collective-permute-start | bytes 4128776 | tf_op jit(solution)/shard_map/ppermute | solution.py:262
  17.4 1.1 copy-start
  88.3 0.7 copy-start.2
  89.1 0.7 copy-start.3
  89.7 20.0 %copy-start.1 = (bf16[16,8,1024]{2,1,0:T(8,128)(2,1)S(1)}, bf16[16,8,1024]{2,1,0:T(8,128)(2,1)}, u32[]{:S(2)}) copy-start(bf16[16,8,1024]{2,1,0:T(8,128)(2,1)} %copy-done) | copy-start | bytes 786436
  89.7 23.6 %all-to-all-start.2 = ((bf16[16,8,512]{2,1,0:T(8,128)(2,1)}), bf16[16,8,512]{2,1,0:T(8,128)(2,1)S(1)}, u32[]{:S(2)}, u32[]{:S(2)}) async-start(bf16[16,8,512]{2,1,0:T(8,128)(2,1)} %bitcast.18), calls=%async_computation.2 | async-start | bytes 262144 | tf_op jit(solution)/shard_map/all_to_all | solution.py:36
